TPU v7x, 256 devices: a whole 4x4x8 slice. The times are simulated.
256 devices in a mesh: src: 8 (over z_lo, x), space: 32 (over y, z_hi, core).
Axes of the slice: x: 4, y: 4, z: 8 (z_hi: 4, z_lo: 2; z = z_hi * 2 + z_lo), core: 2. Of those that a mesh axis runs over, the one named last changes fastest.
Arguments:
- fwd_current: float32 [8, 3, 256, 64, 128], P('src', None, 'space'), may hold values from -6 to 6
- adj_current: float32 [8, 3, 256, 64, 128], P('src', None, 'space'), may hold values from -6 to 6
- inv_eps: float32 [256, 64, 128], P('space'), may hold values from 0.25 to 1
- wavelength: int32 [8], P('src'), may hold values from 0 to 15
- footprint: int32 [256, 64], P('space', 'src'), may hold values from 0 to 4095, as said below
Outputs:
- design_grad: float32 [4096, 128], P(('src', 'space'))
Inputs may be any that keep to these rules, and one draw needn't show every extreme that they name: `footprint`: A column (x, y) whose y lies in the i-th block of 8 cells names a pixel of the pixel blocks i * 32 to (i + 1) * 32 - 1, a pixel block being 16 consecutive pixels. Among the 64 columns of one slab of 8 cells in x and one block in y, at most 4 name pixels of any one pixel block; in each group i one pixel block receives exactly 4 columns from every slab.
All inputs are finite; a program needn't handle non-finite values.
Results may differ from a plain program's by a relative error of at most 0.0003.
Values sent between devices are 32-bit elements; how exact they have to be, the bound alone decides.
No kernel may reach another device: no remote copies, remote signals or barrier semaphores. Data moves between devices by JAX's collectives and lax.ppermute only.
A program may use at most 64 MiB of HBM per device.

v0:
```python
import jax
import jax.numpy as jnp
from jax import lax
from jax.sharding import PartitionSpec as P

ITERS = 4
PIX_DEV = 16


COURANT = 0.5


def passed_along(block, axis, distance):
    devices = range(lax.axis_size(axis))
    route = [(i - distance, i) for i in devices if i - distance in devices]
    return lax.ppermute(block, axis, route)


def roll_fwd(field, axis):
    return jnp.roll(field, -1, axis) - field


def roll_back(field, axis):
    return field - jnp.roll(field, 1, axis)


def curl_electric(parts, ahead):
    grad_y = jnp.concatenate([parts[1][:, 1:], ahead[0]], axis=1) - parts[1]
    grad_z = jnp.concatenate([parts[2][:, 1:], ahead[1]], axis=1) - parts[2]
    return (
        roll_fwd(parts[2], 2) - roll_fwd(parts[1], 3),
        roll_fwd(parts[0], 3) - grad_z,
        grad_y - roll_fwd(parts[0], 2),
    )


def curl_magnetic(parts, behind):
    grad_y = parts[1] - jnp.concatenate([behind[0], parts[1][:, :-1]], axis=1)
    grad_z = parts[2] - jnp.concatenate([behind[1], parts[2][:, :-1]], axis=1)
    return (
        roll_back(parts[2], 2) - roll_back(parts[1], 3),
        roll_back(parts[0], 3) - grad_z,
        grad_y - roll_back(parts[0], 2),
    )


def run_fields(current, signals, inv_eps):
    zero = jnp.zeros((current.shape[0],) + current.shape[2:], jnp.float32)
    electric = (zero, zero, zero)
    magnetic = (zero, zero, zero)
    stored = []
    for step in range(ITERS):
        front = jnp.stack([electric[1][:, 0:1], electric[2][:, 0:1]])
        ahead = passed_along(front, "space", -1)
        curl_e = curl_electric(electric, ahead)
        magnetic = tuple((magnetic[k] - COURANT * curl_e[k] for k in range(3)))
        rear = jnp.stack([magnetic[1][:, -1:], magnetic[2][:, -1:]])
        behind = passed_along(rear, "space", 1)
        curl_h = curl_magnetic(magnetic, behind)
        signal = signals[step][:, None, None, None]
        electric = tuple(
            (
                electric[k] + COURANT * inv_eps[None] * (curl_h[k] - current[:, k] * signal)
                for k in range(3)
            )
        )
        stored.append(electric)
    return stored


def per_device(fwd_current, adj_current, inv_eps, wavelength, footprint):
    omegas = 0.25 + 0.05 * wavelength.astype(jnp.float32)
    sin_signals = [jnp.sin(omegas * (step + 1.0)) for step in range(ITERS)]
    cos_signals = [jnp.cos(omegas * (step + 1.0)) for step in range(ITERS)]
    forward = run_fields(fwd_current, sin_signals, inv_eps)
    adjoint = run_fields(adj_current, cos_signals, inv_eps)
    local_grad = jnp.zeros(inv_eps.shape, jnp.float32)
    for step in range(ITERS):
        for k in range(3):
            local_grad = local_grad + jnp.sum(
                forward[step][k] * adjoint[ITERS - 1 - step][k], axis=0
            )
    summed = lax.psum(local_grad, "src")
    width = footprint.shape[1]
    share = lax.dynamic_slice_in_dim(summed, lax.axis_index("src") * width, width, 1)
    depth = share.shape[2]
    row_count = footprint.shape[0] * footprint.shape[1]
    columns = share.reshape(row_count, depth)
    pixel_ids = footprint.reshape(row_count)
    owners = lax.axis_size("space")
    capacity = max(2, (2 * row_count + owners - 1) // owners)
    target = pixel_ids // PIX_DEV % owners
    onehot = (target[:, None] == jnp.arange(owners, dtype=jnp.int32)[None, :]).astype(jnp.int32)
    ranks = jnp.sum(onehot * (jnp.cumsum(onehot, axis=0) - 1), axis=1)
    slot_of = target * capacity + ranks
    slot_count = owners * capacity
    select = slot_of[None, :] == jnp.arange(slot_count, dtype=jnp.int32)[:, None]
    packed = jnp.dot(
        select.astype(jnp.float32),
        columns,
        preferred_element_type=jnp.float32,
        precision=lax.Precision.HIGHEST,
    )
    packed_ids = jnp.max(jnp.where(select, (pixel_ids % PIX_DEV)[None, :], -1), axis=1)
    arrived, arrived_ids = (
        lax.all_to_all(
            packed.reshape(owners, capacity, depth),
            "space",
            split_axis=0,
            concat_axis=0,
            tiled=True,
        ),
        lax.all_to_all(
            packed_ids.reshape(owners, capacity), "space", split_axis=0, concat_axis=0, tiled=True
        ),
    )
    flat_vals = arrived.reshape(slot_count, depth)
    flat_ids = arrived_ids.reshape(slot_count)
    gather_rows = (flat_ids[None, :] == jnp.arange(PIX_DEV, dtype=jnp.int32)[:, None]).astype(
        jnp.float32
    )
    return jnp.dot(
        gather_rows, flat_vals, preferred_element_type=jnp.float32, precision=lax.Precision.HIGHEST
    )


def solution(mesh):
    in_specs = (
        P("src", None, "space", None, None),
        P("src", None, "space", None, None),
        P("space", None, None),
        P("src"),
        P("space", "src"),
    )
    out_specs = P(("src", "space"), None)
    return jax.shard_map(
        per_device, mesh=mesh, in_specs=in_specs, out_specs=out_specs, check_vma=False
    )
```

profile of v0, /device:TPU:1, one launch (start us, length us, event | category | flops | bytes accessed | tf_op | source)
XLA Modules:
  0.0 199.1 jit_solution(9367090481675807180)
XLA Ops:
  6.5 5.1 %collective-permute-start = (f32[2,1,1,64,128]{4,3,2,1,0:T(8,128)S(1)}, f32[2,1,1,64,128]{4,3,2,1,0:T(8,128)S(1)}, u32[]{:S(2)}, u32[]{:S(2)}) collective-permute-start(f32[2,1,1,64,128]{4,3,2,1,0:T(8,128)S(1)} %broadcast.482), channel_id=1, source_target_pairs={{1,0},{2,1},{3,2},{4,3},{5,4},{6,5},{7,6},{8,7},{9,8},{10,9},{11,1... | collective-permute-start | bytes 196616 | tf_op jit(solution)/shard_map/ppermute | solution.py:16
  13.3 1.5 collective-permute-done
  14.9 1.9 collective-permute-start.1
  17.4 0.8 collective-permute-done.1
  19.3 0.6 copy-done.3
  19.9 0.5 copy-done.1
  21.2 2.5 %collective-permute-start.2 = (f32[2,1,1,64,128]{4,3,2,1,0:T(8,128)S(1)}, f32[2,1,1,64,128]{4,3,2,1,0:T(8,128)S(1)}, u32[]{:S(2)}, u32[]{:S(2)}) collective-permute-start(f32[2,1,1,64,128]{4,3,2,1,0:T(8,128)S(1)} %pad_maximum_fusion.1), channel_id=1, source_target_pairs={{1,0},{2,1},{3,2},{4,3},{5,4},{6,5},{7,6},{8,7},{9,8},{10,9},{11,1... | collective-permute-start | bytes 196616 | tf_op jit(solution)/shard_map/ppermute | solution.py:16
  23.8 1.9 collective-permute-start.8
  25.7 5.3 %collective-permute-done.2 = f32[2,1,1,64,128]{4,3,2,1,0:T(8,128)S(1)} collective-permute-done((f32[2,1,1,64,128]{4,3,2,1,0:T(8,128)S(1)}, f32[2,1,1,64,128]{4,3,2,1,0:T(8,128)S(1)}, u32[]{:S(2)}, u32[]{:S(2)}) %collective-permute-start.2) | collective-permute-done | bytes 65568 | tf_op jit(solution)/shard_map/ppermute | solution.py:16
  31.1 0.4 fusion.15
  31.8 1.1 collective-permute-done.8
  33.0 0.4 fusion.92
  33.8 1.9 collective-permute-start.3
  35.7 6.4 %collective-permute-start.9 = (f32[2,1,1,64,128]{4,3,2,1,0:T(8,128)S(1)}, f32[2,1,1,64,128]{4,3,2,1,0:T(8,128)S(1)}, u32[]{:S(2)}, u32[]{:S(2)}) collective-permute-start(f32[2,1,1,64,128]{4,3,2,1,0:T(8,128)S(1)} %pad_maximum_fusion.8), channel_id=1, source_target_pairs={{0,1},{1,2},{2,3},{3,4},{4,5},{5,6},{6,7},{7,8},{8,9},{9,10},{10,1... | collective-permute-start | bytes 196616 | tf_op jit(solution)/shard_map/ppermute | solution.py:16
  42.1 0.4 fusion.9
  42.8 1.9 collective-permute-start.4
  44.8 0.4 fusion.96
  45.6 4.2 %collective-permute-done.4 = f32[2,1,1,64,128]{4,3,2,1,0:T(8,128)S(1)} collective-permute-done((f32[2,1,1,64,128]{4,3,2,1,0:T(8,128)S(1)}, f32[2,1,1,64,128]{4,3,2,1,0:T(8,128)S(1)}, u32[]{:S(2)}, u32[]{:S(2)}) %collective-permute-start.4) | collective-permute-done | bytes 65568 | tf_op jit(solution)/shard_map/ppermute | solution.py:16
  49.9 0.4 fusion.36
  50.3 1.9 collective-permute-start.5
  52.9 0.6 collective-permute-done.5
  53.6 0.4 fusion.30
  54.2 0.4 fusion.40
  54.9 2.0 collective-permute-start.6
  56.9 1.9 collective-permute-start.10
  58.8 3.2 %collective-permute-done.6 = f32[2,1,1,64,128]{4,3,2,1,0:T(8,128)S(1)} collective-permute-done((f32[2,1,1,64,128]{4,3,2,1,0:T(8,128)S(1)}, f32[2,1,1,64,128]{4,3,2,1,0:T(8,128)S(1)}, u32[]{:S(2)}, u32[]{:S(2)}) %collective-permute-start.6) | collective-permute-done | bytes 65568 | tf_op jit(solution)/shard_map/ppermute | solution.py:16
  62.1 0.4 fusion.47
  62.5 1.5 collective-permute-done.10
  64.0 0.4 fusion.113
  64.5 1.9 collective-permute-start.11
  67.1 0.6 collective-permute-done.11
  68.0 0.4 fusion.107
  68.4 2.0 collective-permute-start.12
  70.4 6.3 %collective-permute-start.7 = (f32[2,1,1,64,128]{4,3,2,1,0:T(8,128)S(1)}, f32[2,1,1,64,128]{4,3,2,1,0:T(8,128)S(1)}, u32[]{:S(2)}, u32[]{:S(2)}) collective-permute-start(f32[2,1,1,64,128]{4,3,2,1,0:T(8,128)S(1)} %pad_maximum_fusion.6), channel_id=1, source_target_pairs={{0,1},{1,2},{2,3},{3,4},{4,5},{5,6},{6,7},{7,8},{8,9},{9,10},{10,1... | collective-permute-start | bytes 196616 | tf_op jit(solution)/shard_map/ppermute | solution.py:16
  77.2 0.4 fusion.124
  77.6 2.6 %collective-permute-start.13 = (f32[2,1,1,64,128]{4,3,2,1,0:T(8,128)S(1)}, f32[2,1,1,64,128]{4,3,2,1,0:T(8,128)S(1)}, u32[]{:S(2)}, u32[]{:S(2)}) collective-permute-start(f32[2,1,1,64,128]{4,3,2,1,0:T(8,128)S(1)} %pad_maximum_fusion.12), channel_id=1, source_target_pairs={{0,1},{1,2},{2,3},{3,4},{4,5},{5,6},{6,7},{7,8},{8,9},{9,10},{10,1... | collective-permute-start | bytes 196616 | tf_op jit(solution)/shard_map/ppermute | solution.py:16
  80.6 0.8 collective-permute-done.13
  81.3 2.2 %fusion.152 = f32[8,64,128]{2,1,0:T(8,128)} fusion(f32[1,8,64,128]{3,2,1,0:T(8,128)S(1)} %copy-done.4, f32[1,8,64,128]{3,2,1,0:T(8,128)S(1)} %get-tuple-element.14, f32[1,8,64,128]{3,2,1,0:T(8,128)S(1)} %get-tuple-element.38, f32[1,8,63,128]{3,2,1,0:T(8,128)S(1)} %bitcast.290, f32[1,8,1,128]{3,2,1,0:T(1,128)S(1)} %slice.1006, ...), kind=kLoop, calls=%fused_computation.239 | loop fusion | flops 5111808 | bytes 11534344 | tf_op jit(solution)/shard_map/add | solution.py:80
  83.7 0.7 all_to_all.9
  84.4 16.7 %all-to-all-start = ((s32[32,1,4]{2,1,0:T(1,128)}), s32[32,1,4]{2,1,0:T(1,128)S(1)}, u32[]{:S(2)}, u32[]{:S(2)}) async-start(s32[32,1,4]{2,1,0:T(1,128)} %bitcast), calls=%async_computation | async-start | bytes 32768 | tf_op jit(solution)/shard_map/all_to_all | solution.py:113
  101.1 64.5 %all-reduce.6.cloned.1.call-done = f32[8,64,128]{2,1,0:T(8,128)} async-done(((f32[8,64,128]{2,1,0:T(8,128)}), f32[8,64,128]{2,1,0:T(8,128)}) %all-reduce.6.cloned.1.call-update) | async-done | bytes 262160 | tf_op jit(solution)/shard_map/psum | solution.py:83
  165.5 1.0 fusion.153
  166.5 0.7 copy.10
  167.2 14.3 %all-to-all-start.1 = ((f32[32,4,128]{2,1,0:T(4,128)}), f32[32,4,128]{2,1,0:T(4,128)S(1)}, u32[]{:S(2)}, u32[]{:S(2)}) async-start(f32[32,4,128]{2,1,0:T(4,128)} %copy.10), calls=%async_computation.1 | async-start | bytes 131072 | tf_op jit(solution)/shard_map/all_to_all | solution.py:106
  181.5 0.5 broadcast.585
  182.0 0.7 reduce.3
  182.8 8.6 %all-to-all-done.1 = f32[32,4,128]{2,1,0:T(4,128)S(1)} async-done(((f32[32,4,128]{2,1,0:T(4,128)}), f32[32,4,128]{2,1,0:T(4,128)S(1)}, u32[]{:S(2)}, u32[]{:S(2)}) %all-to-all-start.1) | async-done | bytes 65568 | tf_op jit(solution)/shard_map/all_to_all | solution.py:106
  191.5 0.8 fusion.160
  (180 shorter events, 6.7 us)
Async XLA Ops:
  6.5 5.2 %copy-start.5 = (s32[8,8]{1,0:T(8,128)S(1)}, s32[8,8]{1,0:T(8,128)}, u32[]{:S(2)}) copy-start(s32[8,8]{1,0:T(8,128)} %param.9) | copy-start | bytes 772
  6.5 159.0 %all-reduce.6.cloned.1.call-start = ((), (), s32[]{:S(2)}) async-start(), calls=%async_computation.2 | async-start | bytes 524288 | tf_op jit(solution)/shard_map/psum | solution.py:83
  6.5 8.2 %collective-permute-start = (f32[2,1,1,64,128]{4,3,2,1,0:T(8,128)S(1)}, f32[2,1,1,64,128]{4,3,2,1,0:T(8,128)S(1)}, u32[]{:S(2)}, u32[]{:S(2)}) collective-permute-start(f32[2,1,1,64,128]{4,3,2,1,0:T(8,128)S(1)} %broadcast.482), channel_id=1, source_target_pairs={{1,0},{2,1},{3,2},{4,3},{5,4},{6,5},{7,6},{8,7},{9,8},{10,9},{11,1... | collective-permute-start | bytes 196616 | tf_op jit(solution)/shard_map/ppermute | solution.py:16
  14.9 3.2 %collective-permute-start.1 = (f32[2,1,1,64,128]{4,3,2,1,0:T(8,128)S(1)}, f32[2,1,1,64,128]{4,3,2,1,0:T(8,128)S(1)}, u32[]{:S(2)}, u32[]{:S(2)}) collective-permute-start(f32[2,1,1,64,128]{4,3,2,1,0:T(8,128)S(1)} %pad_maximum_fusion), channel_id=1, source_target_pairs={{0,1},{1,2},{2,3},{3,4},{4,5},{5,6},{6,7},{7,8},{8,9},{9,10},{10,1... | collective-permute-start | bytes 196616 | tf_op jit(solution)/shard_map/ppermute | solution.py:16
  17.2 1.1 copy-start.2
  17.3 1.1 copy-start
  19.2 0.7 copy-start.3
  19.2 1.2 copy-start.1
  21.1 9.9 %copy-start.4 = (f32[1,8,64,128]{3,2,1,0:T(8,128)S(1)}, f32[1,8,64,128]{3,2,1,0:T(8,128)}, u32[]{:S(2)}) copy-start(f32[1,8,64,128]{3,2,1,0:T(8,128)} %copy-done.3) | copy-start | bytes 786436
  21.2 9.9 %slice-start = ((f32[1,8,64,128]{3,2,1,0:T(8,128)}), f32[1,7,64,128]{3,2,1,0:T(8,128)S(1)}, s32[]{:S(2)}) async-start(f32[1,8,64,128]{3,2,1,0:T(8,128)} %copy-done.3), calls=%async_computation.3 | async-start | bytes 458752 | tf_op jit(solution)/shard_map/slice | solution.py:29
  21.2 9.8 %collective-permute-start.2 = (f32[2,1,1,64,128]{4,3,2,1,0:T(8,128)S(1)}, f32[2,1,1,64,128]{4,3,2,1,0:T(8,128)S(1)}, u32[]{:S(2)}, u32[]{:S(2)}) collective-permute-start(f32[2,1,1,64,128]{4,3,2,1,0:T(8,128)S(1)} %pad_maximum_fusion.1), channel_id=1, source_target_pairs={{1,0},{2,1},{3,2},{4,3},{5,4},{6,5},{7,6},{8,7},{9,8},{10,9},{11,1... | collective-permute-start | bytes 196616 | tf_op jit(solution)/shard_map/ppermute | solution.py:16
  23.8 9.2 %collective-permute-start.8 = (f32[2,1,1,64,128]{4,3,2,1,0:T(8,128)S(1)}, f32[2,1,1,64,128]{4,3,2,1,0:T(8,128)S(1)}, u32[]{:S(2)}, u32[]{:S(2)}) collective-permute-start(f32[2,1,1,64,128]{4,3,2,1,0:T(8,128)S(1)} %pad_maximum_fusion.7), channel_id=1, source_target_pairs={{1,0},{2,1},{3,2},{4,3},{5,4},{6,5},{7,6},{8,7},{9,8},{10,9},{11,1... | collective-permute-start | bytes 196616 | tf_op jit(solution)/shard_map/ppermute | solution.py:16
  33.8 8.3 %collective-permute-start.3 = (f32[2,1,1,64,128]{4,3,2,1,0:T(8,128)S(1)}, f32[2,1,1,64,128]{4,3,2,1,0:T(8,128)S(1)}, u32[]{:S(2)}, u32[]{:S(2)}) collective-permute-start(f32[2,1,1,64,128]{4,3,2,1,0:T(8,128)S(1)} %pad_maximum_fusion.2), channel_id=1, source_target_pairs={{0,1},{1,2},{2,3},{3,4},{4,5},{5,6},{6,7},{7,8},{8,9},{9,10},{10,1... | collective-permute-start | bytes 196616 | tf_op jit(solution)/shard_map/ppermute | solution.py:16
  35.7 9.0 %collective-permute-start.9 = (f32[2,1,1,64,128]{4,3,2,1,0:T(8,128)S(1)}, f32[2,1,1,64,128]{4,3,2,1,0:T(8,128)S(1)}, u32[]{:S(2)}, u32[]{:S(2)}) collective-permute-start(f32[2,1,1,64,128]{4,3,2,1,0:T(8,128)S(1)} %pad_maximum_fusion.8), channel_id=1, source_target_pairs={{0,1},{1,2},{2,3},{3,4},{4,5},{5,6},{6,7},{7,8},{8,9},{9,10},{10,1... | collective-permute-start | bytes 196616 | tf_op jit(solution)/shard_map/ppermute | solution.py:16
  42.8 7.0 %collective-permute-start.4 = (f32[2,1,1,64,128]{4,3,2,1,0:T(8,128)S(1)}, f32[2,1,1,64,128]{4,3,2,1,0:T(8,128)S(1)}, u32[]{:S(2)}, u32[]{:S(2)}) collective-permute-start(f32[2,1,1,64,128]{4,3,2,1,0:T(8,128)S(1)} %pad_maximum_fusion.3), channel_id=1, source_target_pairs={{1,0},{2,1},{3,2},{4,3},{5,4},{6,5},{7,6},{8,7},{9,8},{10,9},{11,1... | collective-permute-start | bytes 196616 | tf_op jit(solution)/shard_map/ppermute | solution.py:16
  50.3 3.2 %collective-permute-start.5 = (f32[2,1,1,64,128]{4,3,2,1,0:T(8,128)S(1)}, f32[2,1,1,64,128]{4,3,2,1,0:T(8,128)S(1)}, u32[]{:S(2)}, u32[]{:S(2)}) collective-permute-start(f32[2,1,1,64,128]{4,3,2,1,0:T(8,128)S(1)} %pad_maximum_fusion.4), channel_id=1, source_target_pairs={{0,1},{1,2},{2,3},{3,4},{4,5},{5,6},{6,7},{7,8},{8,9},{9,10},{10,1... | collective-permute-start | bytes 196616 | tf_op jit(solution)/shard_map/ppermute | solution.py:16
  54.9 7.2 %collective-permute-start.6 = (f32[2,1,1,64,128]{4,3,2,1,0:T(8,128)S(1)}, f32[2,1,1,64,128]{4,3,2,1,0:T(8,128)S(1)}, u32[]{:S(2)}, u32[]{:S(2)}) collective-permute-start(f32[2,1,1,64,128]{4,3,2,1,0:T(8,128)S(1)} %pad_maximum_fusion.5), channel_id=1, source_target_pairs={{1,0},{2,1},{3,2},{4,3},{5,4},{6,5},{7,6},{8,7},{9,8},{10,9},{11,1... | collective-permute-start | bytes 196616 | tf_op jit(solution)/shard_map/ppermute | solution.py:16
  56.9 7.1 %collective-permute-start.10 = (f32[2,1,1,64,128]{4,3,2,1,0:T(8,128)S(1)}, f32[2,1,1,64,128]{4,3,2,1,0:T(8,128)S(1)}, u32[]{:S(2)}, u32[]{:S(2)}) collective-permute-start(f32[2,1,1,64,128]{4,3,2,1,0:T(8,128)S(1)} %pad_maximum_fusion.9), channel_id=1, source_target_pairs={{1,0},{2,1},{3,2},{4,3},{5,4},{6,5},{7,6},{8,7},{9,8},{10,9},{11,1... | collective-permute-start | bytes 196616 | tf_op jit(solution)/shard_map/ppermute | solution.py:16
  64.5 3.2 %collective-permute-start.11 = (f32[2,1,1,64,128]{4,3,2,1,0:T(8,128)S(1)}, f32[2,1,1,64,128]{4,3,2,1,0:T(8,128)S(1)}, u32[]{:S(2)}, u32[]{:S(2)}) collective-permute-start(f32[2,1,1,64,128]{4,3,2,1,0:T(8,128)S(1)} %pad_maximum_fusion.10), channel_id=1, source_target_pairs={{0,1},{1,2},{2,3},{3,4},{4,5},{5,6},{6,7},{7,8},{8,9},{9,10},{10,1... | collective-permute-start | bytes 196616 | tf_op jit(solution)/shard_map/ppermute | solution.py:16
  68.4 8.7 %collective-permute-start.12 = (f32[2,1,1,64,128]{4,3,2,1,0:T(8,128)S(1)}, f32[2,1,1,64,128]{4,3,2,1,0:T(8,128)S(1)}, u32[]{:S(2)}, u32[]{:S(2)}) collective-permute-start(f32[2,1,1,64,128]{4,3,2,1,0:T(8,128)S(1)} %pad_maximum_fusion.11), channel_id=1, source_target_pairs={{1,0},{2,1},{3,2},{4,3},{5,4},{6,5},{7,6},{8,7},{9,8},{10,9},{11,1... | collective-permute-start | bytes 196616 | tf_op jit(solution)/shard_map/ppermute | solution.py:16
  70.4 9.8 %collective-permute-start.7 = (f32[2,1,1,64,128]{4,3,2,1,0:T(8,128)S(1)}, f32[2,1,1,64,128]{4,3,2,1,0:T(8,128)S(1)}, u32[]{:S(2)}, u32[]{:S(2)}) collective-permute-start(f32[2,1,1,64,128]{4,3,2,1,0:T(8,128)S(1)} %pad_maximum_fusion.6), channel_id=1, source_target_pairs={{0,1},{1,2},{2,3},{3,4},{4,5},{5,6},{6,7},{7,8},{8,9},{9,10},{10,1... | collective-permute-start | bytes 196616 | tf_op jit(solution)/shard_map/ppermute | solution.py:16
  77.6 3.7 %collective-permute-start.13 = (f32[2,1,1,64,128]{4,3,2,1,0:T(8,128)S(1)}, f32[2,1,1,64,128]{4,3,2,1,0:T(8,128)S(1)}, u32[]{:S(2)}, u32[]{:S(2)}) collective-permute-start(f32[2,1,1,64,128]{4,3,2,1,0:T(8,128)S(1)} %pad_maximum_fusion.12), channel_id=1, source_target_pairs={{0,1},{1,2},{2,3},{3,4},{4,5},{5,6},{6,7},{7,8},{8,9},{9,10},{10,1... | collective-permute-start | bytes 196616 | tf_op jit(solution)/shard_map/ppermute | solution.py:16
  84.4 82.8 %all-to-all-start = ((s32[32,1,4]{2,1,0:T(1,128)}), s32[32,1,4]{2,1,0:T(1,128)S(1)}, u32[]{:S(2)}, u32[]{:S(2)}) async-start(s32[32,1,4]{2,1,0:T(1,128)} %bitcast), calls=%async_computation | async-start | bytes 32768 | tf_op jit(solution)/shard_map/all_to_all | solution.py:113
  167.2 24.3 %all-to-all-start.1 = ((f32[32,4,128]{2,1,0:T(4,128)}), f32[32,4,128]{2,1,0:T(4,128)S(1)}, u32[]{:S(2)}, u32[]{:S(2)}) async-start(f32[32,4,128]{2,1,0:T(4,128)} %copy.10), calls=%async_computation.1 | async-start | bytes 131072 | tf_op jit(solution)/shard_map/all_to_all | solution.py:106
Sparse Core Ops, SparseCore 0:
  83.7 81.8 all-reduce.5
where the time goes:
time: 200 us; the launch traced here: 199 us
  waiting for transfers between devices  92.8 us (46%)
  starting transfers between devices  71.4 us (36%)
  between operations  16.1 us (8%)
  other arithmetic  9.26 us (5%)
  local copies, waits for them, and re-layouts  7.8 us (4%)
    psum x1, waiting for transfers between devices, per_device(): summed = lax.psum(local_grad, 'src')  64.5 us
    ppermute x14, starting transfers between devices, passed_along(): return lax.ppermute(block, axis, route)  40.4 us
    ppermute x14, waiting for transfers between devices, passed_along(): return lax.ppermute(block, axis, route)  19.7 us
    all_to_all x1, starting transfers between devices, per_device(): lax.all_to_all(packed_ids.reshape(owners, capacity), 'space', split_axis=...  16.7 us
    all_to_all x1, starting transfers between devices, per_device(): lax.all_to_all(packed.reshape(owners, capacity, depth), 'space', split_ax...  14.3 us
    all_to_all x1, waiting for transfers between devices, per_device(): lax.all_to_all(packed.reshape(owners, capacity, depth), 'space', split_ax...  8.63 us
  transfers between devices with their start and end apart: 17, of which 12 were waited for; matrix products, arithmetic and copies ran while one was open for 4% of the time, Pallas kernels for 0%

commit v1 on v0

v1 whole, which is shorter than its diff:
```python
import jax
import jax.numpy as jnp
from jax import lax
from jax.experimental import pallas as pl
from jax.experimental.pallas import tpu as pltpu
from jax.sharding import PartitionSpec as P

ITERS = 4
PIX_DEV = 16
CAP = 4
F32 = jnp.float32


def y_next(a):
    return pltpu.roll(a, a.shape[0] - 1, 0)


def y_prev(a):
    return pltpu.roll(a, 1, 0)


def z_next(a):
    return pltpu.roll(a, a.shape[1] - 1, 1)


def z_prev(a):
    return pltpu.roll(a, 1, 1)


def curl_f(v, v2_next, v3_next):
    v1, v2, v3 = v
    h1 = (y_next(v3) - v3) - (z_next(v2) - v2)
    h2 = (z_next(v1) - v1) - (v3_next - v3)
    h3 = (v2_next - v2) - (y_next(v1) - v1)
    return h1, h2, h3


def scaled_curl_b(h, h2_prev, h3_prev, e):
    h1, h2, h3 = h
    return (
        e * ((h3 - y_prev(h3)) - (h2 - z_prev(h2))),
        e * ((h1 - z_prev(h1)) - (h3 - h3_prev)),
        e * ((h2 - h2_prev) - (h1 - y_prev(h1))),
    )


def edge_kernel(fwd, adj, eps, to_next, to_prev):
    last = eps.shape[0] - 1
    for run, current in enumerate((fwd, adj)):
        def source(i):
            e = -0.25 * eps[i]
            return tuple(e * current[0, c, i] for c in range(3))

        def put_next(k, v):
            to_next[run * 6 + k * 2] = v[2] + (z_next(v[0]) - v[0])
            to_next[run * 6 + k * 2 + 1] = v[1] + (y_next(v[0]) - v[0])

        def put_prev(k, v):
            to_prev[run * 6 + k * 2] = v[1]
            to_prev[run * 6 + k * 2 + 1] = v[2]

        a, b, c = source(last - 2), source(last - 1), source(last)
        put_next(0, c)
        zero = jnp.zeros_like(c[0])
        ha = curl_f(a, b[1], b[2])
        hb = curl_f(b, c[1], c[2])
        hc = curl_f(c, zero, zero)
        b = scaled_curl_b(hb, ha[1], ha[2], -0.25 * eps[last - 1])
        c = scaled_curl_b(hc, hb[1], hb[2], -0.25 * eps[last])
        put_next(1, c)
        hb = curl_f(b, c[1], c[2])
        hc = curl_f(c, zero, zero)
        put_next(2, scaled_curl_b(hc, hb[1], hb[2], -0.25 * eps[last]))

        a, b, c = source(0), source(1), source(2)
        put_prev(0, a)
        ha = curl_f(a, b[1], b[2])
        hb = curl_f(b, c[1], c[2])
        a1 = scaled_curl_b(ha, -a[2], a[1], -0.25 * eps[0])
        b1 = scaled_curl_b(hb, ha[1], ha[2], -0.25 * eps[1])
        put_prev(1, a1)
        ha = curl_f(a1, b1[1], b1[2])
        put_prev(2, scaled_curl_b(ha, -a1[2], a1[1], -0.25 * eps[0]))
    to_next[12] = -0.25 * eps[last]
    to_prev[12] = -0.25 * eps[0]


def pair_factors(sig):
    def by_step(s):
        s1, s2, s3, s4 = s
        return (
            (s1,),
            (s1 + s2, s1),
            (s1 + s2 + s3, 3.0 * s1 + s2, s1),
            (s1 + s2 + s3 + s4, 6.0 * s1 + 3.0 * s2 + s3, 5.0 * s1 + s2, s1),
        )

    f = by_step([sig[i] for i in range(ITERS)])
    a = by_step([sig[ITERS + i] for i in range(ITERS)])
    factors = {}
    for t in range(ITERS):
        for k, fk in enumerate(f[t]):
            for m, am in enumerate(a[ITERS - 1 - t]):
                factors[k, m] = factors.get((k, m), 0.0) + 4.0 * fk * am
    return factors


def field_kernel(sig, fwd, adj, eps, from_prev, from_next, out, v):
    planes = eps.shape[0]
    has_prev, has_next = sig[8], sig[9]
    e_prev, e_next = from_prev[12] * has_prev, from_next[12] * has_next
    factors = pair_factors(sig)

    def start(i, _):
        e = -0.25 * eps[i]
        for run, current in enumerate((fwd, adj)):
            for c in range(3):
                v[0, run, c, i] = e * current[0, c, i]
        return 0

    lax.fori_loop(0, planes, start, 0)
    zero = jnp.zeros(eps.shape[1:], F32)
    before = [(zero,) * 3, (zero,) * 3]
    after = [(zero,) * 3, (zero,) * 3]

    def read(k, run, i):
        return tuple(v[k, run, c, i] for c in range(3))

    for k in range(3):
        behind = []
        for run in range(2):
            c = before[run]
            h = curl_f(c, v[k, run, 1, 0], v[k, run, 2, 0])
            if k < 2:
                before[run] = scaled_curl_b(h, -c[2], c[1], e_prev)
            row = run * 6 + k * 2
            behind += [(h[1] + from_prev[row]) * has_prev, (h[2] - from_prev[row + 1]) * has_prev]

        def finish(i, new):
            if k < 2:
                for run in range(2):
                    for c in range(3):
                        v[k + 1, run, c, i] = new[run][c]
                return
            total = None
            for c in range(3):
                f = [v[j, 0, c, i] for j in range(3)] + [new[0][c]]
                a = [v[j, 1, c, i] for j in range(3)] + [new[1][c]]
                for m in range(4):
                    mix = None
                    for j in range(4 - m):
                        term = factors[j, m] * f[j]
                        mix = term if mix is None else mix + term
                    total = mix * a[m] if total is None else total + mix * a[m]
            for block in range(out.shape[0]):
                out[block, i] = total[block * 8 : block * 8 + 8]

        def plane(i, carry):
            e = -0.25 * eps[i]
            new, left = [], []
            for run in range(2):
                h = curl_f(read(k, run, i), v[k, run, 1, i + 1], v[k, run, 2, i + 1])
                new.append(scaled_curl_b(h, carry[2 * run], carry[2 * run + 1], e))
                left += [h[1], h[2]]
            finish(i, new)
            return tuple(left)

        carry = lax.fori_loop(0, planes - 1, plane, tuple(behind))
        last, new = planes - 1, []
        for run in range(2):
            d = after[run]
            own = curl_f(read(k, run, last), d[1], d[2])
            row = run * 6 + k * 2
            h = (own[0], own[1] - from_next[row + 1] * has_next, own[2] + from_next[row] * has_next)
            new.append(scaled_curl_b(h, carry[2 * run], carry[2 * run + 1], -0.25 * eps[last]))
            if k < 2:
                after[run] = scaled_curl_b(curl_f(d, zero, zero), own[1], own[2], e_next)
        finish(last, new)


def pack_kernel(owners, parts, fp_row, fp_col, out):
    count = parts.shape[1]
    summed = parts[0]
    for s in range(1, parts.shape[0]):
        summed = summed + parts[s]
    row_owner = (fp_row[...] >> 4) & (owners - 1)
    col_owner = (fp_col[...] >> 4) & (owners - 1)
    earlier = lax.broadcasted_iota(jnp.int32, (count, count), 0) < lax.broadcasted_iota(
        jnp.int32, (count, count), 1
    )
    same = (row_owner == col_owner) & earlier
    rank = jnp.sum(same.astype(jnp.int32), axis=0, keepdims=True)
    slot = row_owner * (2 * CAP) + rank
    rows = lax.broadcasted_iota(jnp.int32, (out.shape[0], count), 0)
    put = jnp.concatenate([(rows == slot).astype(F32), (rows == slot + CAP).astype(F32)], axis=1)
    pixel = (
        (fp_col[...] & (PIX_DEV - 1)) == lax.broadcasted_iota(jnp.int32, (count, summed.shape[1]), 1)
    ).astype(F32)
    out[...] = jnp.dot(
        put,
        jnp.concatenate([summed, pixel], axis=0),
        preferred_element_type=F32,
        precision=lax.Precision.HIGHEST,
    )


def pixel_kernel(arrived, out):
    got = arrived[...]
    rows = lax.broadcasted_iota(jnp.int32, got.shape, 0)
    is_data = (rows & (2 * CAP - 1)) < CAP
    pixel = jnp.where(is_data, pltpu.roll(got, got.shape[0] - CAP, 0), 0.0)
    sums = lax.dot_general(
        pixel,
        got,
        (((0,), (0,)), ((), ())),
        preferred_element_type=F32,
        precision=lax.Precision.HIGHEST,
    )
    out[...] = sums[: out.shape[0]]


def per_device(fwd_current, adj_current, inv_eps, wavelength, footprint):
    planes, ny, nz = inv_eps.shape
    space = lax.axis_size("space")
    groups = lax.axis_size("src")
    omega = 0.25 + 0.05 * wavelength.astype(F32)
    phases = omega * (jnp.arange(ITERS, dtype=F32) + 1.0)
    here = lax.axis_index("space")
    edges = jnp.stack([here > 0, here < space - 1]).astype(F32)
    sig = jnp.concatenate([jnp.sin(phases), jnp.cos(phases), edges])

    vmem = pl.BlockSpec(memory_space=pltpu.VMEM)
    smem = pl.BlockSpec(memory_space=pltpu.SMEM)
    trace = jax.ShapeDtypeStruct((13, ny, nz), F32)
    to_next, to_prev = pl.pallas_call(
        edge_kernel, out_shape=(trace, trace), in_specs=[vmem] * 3, out_specs=(vmem, vmem)
    )(fwd_current, adj_current, inv_eps)
    from_prev = lax.ppermute(to_next, "space", [(i, (i + 1) % space) for i in range(space)])
    from_next = lax.ppermute(to_prev, "space", [((i + 1) % space, i) for i in range(space)])
    width = ny // groups
    grad = pl.pallas_call(
        field_kernel,
        out_shape=jax.ShapeDtypeStruct((groups, planes, width, nz), F32),
        in_specs=[smem] + [vmem] * 5,
        out_specs=vmem,
        scratch_shapes=[pltpu.VMEM((3, 2, 3, planes, ny, nz), F32)],
        compiler_params=pltpu.CompilerParams(vmem_limit_bytes=48 * 1024 * 1024),
    )(sig, fwd_current, adj_current, inv_eps, from_prev, from_next)
    count = planes * width
    parts = lax.all_to_all(grad.reshape(groups, count, nz), "src", 0, 0, tiled=True)
    packed = pl.pallas_call(
        lambda *refs: pack_kernel(space, *refs),
        out_shape=jax.ShapeDtypeStruct((space * 2 * CAP, nz), F32),
        in_specs=[vmem] * 3,
        out_specs=vmem,
    )(parts, footprint.reshape(1, count), footprint.reshape(count, 1))
    arrived = lax.all_to_all(packed.reshape(space, 2 * CAP, nz), "space", 0, 0, tiled=True)
    return pl.pallas_call(
        pixel_kernel,
        out_shape=jax.ShapeDtypeStruct((PIX_DEV, nz), F32),
        in_specs=[vmem],
        out_specs=vmem,
    )(arrived.reshape(space * 2 * CAP, nz))


def solution(mesh):
    in_specs = (
        P("src", None, "space", None, None),
        P("src", None, "space", None, None),
        P("space", None, None),
        P("src"),
        P("space", "src"),
    )
    out_specs = P(("src", "space"), None)
    return jax.shard_map(
        per_device, mesh=mesh, in_specs=in_specs, out_specs=out_specs, check_vma=False
    )
```

time: 200 us -> 64.8 us (0.32)
  waiting for transfers between devices: 92.8 us -> 17.3 us
  starting transfers between devices: 71.4 us -> 8.54 us
  blocking collectives: 0 us -> 22.3 us
  between operations: 16.1 us -> 0.68 us
  Pallas kernels: 0 us -> 13.5 us
  other arithmetic: 9.26 us -> 0.2 us
  local copies, waits for them, and re-layouts: 7.8 us -> 2.01 us
    psum x1 -> x0, waiting for transfers between devices: 64.5 us -> none  [per_device(): summed = lax.psum(local_grad, 'src')]
    ppermute x14 -> x2, starting transfers between devices: 40.4 us -> 4.38 us  [the longest x1 4.38 us: per_device(): lax.ppermute(to_next, 'space', [(i, (i + 1) % space) for i in range(space)])]
    all_to_all x2 -> x1, starting transfers between devices: 31 us -> 4.15 us  [per_device(): lax.all_to_all(grad.reshape(groups, count, nz), 'src', 0, 0, tiled=True)]
    all_to_all x0 -> x1, blocking collectives: none -> 22.3 us  [per_device(): lax.all_to_all(packed.reshape(space, 2 * CAP, nz), 'space', 0, 0, tiled=T...]
    pallas_call x0 -> x4, Pallas kernels: none -> 13.5 us  [the longest x1 6.36 us: per_device(): pl.pallas_call(field_kernel, out_shape=jax.ShapeDtypeStruct((groups, plan...]
    ppermute x14 -> x2, waiting for transfers between devices: 19.7 us -> 12.5 us  [the longest x1 6.9 us: per_device(): lax.ppermute(to_prev, 'space', [((i + 1) % space, i) for i in range(space)])]
    add x9 -> x0, other arithmetic: 4.73 us -> none  [the longest x7 2.54 us: run_fields(): electric[k] + COURANT * inv_eps[None] * (curl_h[k] - current[:, k] * signal)]
    slice x93 -> x0, local copies, waits for them, and re-layouts: 4.13 us -> none  [the longest x28 1.85 us: roll_back(): return field - jnp.roll(field, 1, axis)]
  transfers between devices with their start and end apart: 17 -> 3, of which waited for: 12 -> 3; matrix products, arithmetic and copies ran while one was open for 4% -> 2% of each run, Pallas kernels for 0% -> 0%
where the time goes in v1:
time: 64.8 us; the launch traced here: 64.5 us
  blocking collectives  22.3 us (34%)
  waiting for transfers between devices  17.3 us (27%)
  Pallas kernels  13.5 us (21%)
  starting transfers between devices  8.54 us (13%)
  local copies, waits for them, and re-layouts  2.01 us (3%)
  between operations  0.68 us (1%)
    all_to_all x1, blocking collectives, per_device(): lax.all_to_all(packed.reshape(space, 2 * CAP, nz), 'space', 0, 0, tiled=T...  22.3 us
    ppermute x1, waiting for transfers between devices, per_device(): lax.ppermute(to_prev, 'space', [((i + 1) % space, i) for i in range(space)])  6.9 us
    pallas_call x1, Pallas kernels, per_device(): pl.pallas_call(field_kernel, out_shape=jax.ShapeDtypeStruct((groups, plan...  6.36 us
    ppermute x1, waiting for transfers between devices, per_device(): lax.ppermute(to_next, 'space', [(i, (i + 1) % space) for i in range(space)])  5.57 us
    all_to_all x1, waiting for transfers between devices, per_device(): lax.all_to_all(grad.reshape(groups, count, nz), 'src', 0, 0, tiled=True)  4.79 us
    ppermute x1, starting transfers between devices, per_device(): lax.ppermute(to_next, 'space', [(i, (i + 1) % space) for i in range(space)])  4.38 us
    all_to_all x1, starting transfers between devices, per_device(): lax.all_to_all(grad.reshape(groups, count, nz), 'src', 0, 0, tiled=True)  4.15 us
    pallas_call x1, Pallas kernels, per_device(): pl.pallas_call(edge_kernel, out_shape=(trace, trace), in_specs=[vmem] * 3...  3.31 us
  transfers between devices with their start and end apart: 3, of which 3 were waited for; matrix products, arithmetic and copies ran while one was open for 2% of the time, Pallas kernels for 0%

profile of v1, /device:TPU:1, one launch (start us, length us, event | category | flops | bytes accessed | tf_op | source)
XLA Modules:
  0.0 64.5 jit_solution(266597245192474897)
XLA Ops:
  0.0 0.0 copy-start
  0.0 0.0 copy-start.1
  0.0 0.0 copy-start.2
  0.0 3.3 %shard_map.55 = (f32[13,64,128]{2,1,0:T(8,128)}, f32[13,64,128]{2,1,0:T(8,128)}) custom-call(f32[1,3,8,64,128]{4,3,2,1,0:T(8,128)} %fwd.3, f32[1,3,8,64,128]{4,3,2,1,0:T(8,128)} %adj.3, f32[8,64,128]{2,1,0:T(8,128)} %eps.3), custom_call_target="tpu_custom_call" | custom-call | tf_op jit(solution)/shard_map/pallas_call | solution.py:235
  3.3 4.4 %collective-permute-start = (f32[13,64,128]{2,1,0:T(8,128)}, f32[13,64,128]{2,1,0:T(8,128)S(1)}, u32[]{:S(2)}, u32[]{:S(2)}) collective-permute-start(f32[13,64,128]{2,1,0:T(8,128)} %get-tuple-element.7), channel_id=1, source_target_pairs={{0,1},{1,2},{2,3},{3,4},{4,5},{5,6},{6,7},{7,8},{8,9},{9,10},{10,1... | collective-permute-start | bytes 1277960 | tf_op jit(solution)/shard_map/ppermute | solution.py:238
  7.7 0.0 collective-permute-start.1
  8.4 0.1 add_convert_fusion
  8.5 0.1 pad_maximum_fusion.sig
  8.6 5.6 %collective-permute-done.from_prev = f32[13,64,128]{2,1,0:T(8,128)S(1)} collective-permute-done((f32[13,64,128]{2,1,0:T(8,128)}, f32[13,64,128]{2,1,0:T(8,128)S(1)}, u32[]{:S(2)}, u32[]{:S(2)}) %collective-permute-start) | collective-permute-done | bytes 426016 | tf_op jit(solution)/shard_map/ppermute | solution.py:238
  14.1 6.9 %collective-permute-done.1.from_next = f32[13,64,128]{2,1,0:T(8,128)S(1)} collective-permute-done((f32[13,64,128]{2,1,0:T(8,128)}, f32[13,64,128]{2,1,0:T(8,128)S(1)}, u32[]{:S(2)}, u32[]{:S(2)}) %collective-permute-start.1) | collective-permute-done | bytes 426016 | tf_op jit(solution)/shard_map/ppermute | solution.py:239
  21.0 0.0 copy-done
  21.0 0.0 copy-done.1
  21.0 0.0 copy-done.2
  21.0 6.4 %shard_map.56 = f32[8,8,8,128]{3,2,1,0:T(8,128)} custom-call(f32[10]{0:T(128)S(1)} %pad_maximum_fusion.sig, f32[1,3,8,64,128]{4,3,2,1,0:T(8,128)S(1)} %copy-done, f32[1,3,8,64,128]{4,3,2,1,0:T(8,128)S(1)} %copy-done.1, f32[8,64,128]{2,1,0:T(8,128)S(1)} %copy-done.2, f32[13,64,128]{2,1,0:T(8,128)S(1)} %collective-permute-done.from_prev, ...), custom_call_target="tpu_custom_call" | custom-call | tf_op jit(solution)/shard_map/pallas_call | solution.py:241
  27.4 0.0 copy-start.4
  27.4 4.2 %all-to-all-start = ((f32[8,64,128]{2,1,0:T(8,128)}), f32[8,64,128]{2,1,0:T(8,128)S(1)}, u32[]{:S(2)}, u32[]{:S(2)}) async-start(f32[8,64,128]{2,1,0:T(8,128)} %bitcast.3), calls=%async_computation | async-start | bytes 524288 | tf_op jit(solution)/shard_map/all_to_all | solution.py:250
  31.6 0.0 copy-done.4
  31.6 0.7 %reshape.20.refs_2_ = s32[64,1]{1,0:T(8,128)} reshape(s32[8,8]{1,0:T(8,128)S(1)} %copy-done.4) | data formatting | bytes 512 | tf_op jit(solution)/shard_map/reshape | solution.py:256
  32.3 0.6 reshape.16.refs_1_
  32.9 4.8 %all-to-all-done.refs_0_ = f32[8,64,128]{2,1,0:T(8,128)S(1)} async-done(((f32[8,64,128]{2,1,0:T(8,128)}), f32[8,64,128]{2,1,0:T(8,128)S(1)}, u32[]{:S(2)}, u32[]{:S(2)}) %all-to-all-start) | async-done | bytes 262176 | tf_op jit(solution)/shard_map/all_to_all | solution.py:250
  37.6 0.0 copy-start.3
  37.6 0.7 %copy-done.3 = f32[8,64,128]{2,1,0:T(8,128)} copy-done((f32[8,64,128]{2,1,0:T(8,128)}, f32[8,64,128]{2,1,0:T(8,128)S(1)}, u32[]{:S(2)}) %copy-start.3) | copy-done | bytes 262168
  38.4 2.0 %shard_map.57 = f32[256,128]{1,0:T(8,128)} custom-call(f32[8,64,128]{2,1,0:T(8,128)} %copy-done.3, s32[1,64]{1,0:T(1,128)} %reshape.16.refs_1_, s32[64,1]{1,0:T(8,128)} %reshape.20.refs_2_), custom_call_target="tpu_custom_call" | custom-call | tf_op jit(solution)/shard_map/pallas_call | solution.py:251
  40.4 22.3 %all_to_all.10 = f32[32,8,128]{2,1,0:T(8,128)} all-to-all(f32[32,8,128]{2,1,0:T(8,128)} %bitcast.7), channel_id=1, replica_groups=mesh['src'=8,'space'=32] {'space'}, dimensions={0} | all-to-all | bytes 262144 | tf_op jit(solution)/shard_map/all_to_all | solution.py:257
  62.7 1.8 %shard_map.58 = f32[16,128]{1,0:T(8,128)} custom-call(f32[256,128]{1,0:T(8,128)} %bitcast.6), custom_call_target="tpu_custom_call" | custom-call | tf_op jit(solution)/shard_map/pallas_call | solution.py:258
  (1 shorter events, 0.0 us)
Async XLA Ops:
  0.0 21.0 %copy-start = (f32[1,3,8,64,128]{4,3,2,1,0:T(8,128)S(1)}, f32[1,3,8,64,128]{4,3,2,1,0:T(8,128)}, u32[]{:S(2)}) copy-start(f32[1,3,8,64,128]{4,3,2,1,0:T(8,128)} %fwd.3) | copy-start | bytes 2359300
  0.0 21.0 %copy-start.1 = (f32[1,3,8,64,128]{4,3,2,1,0:T(8,128)S(1)}, f32[1,3,8,64,128]{4,3,2,1,0:T(8,128)}, u32[]{:S(2)}) copy-start(f32[1,3,8,64,128]{4,3,2,1,0:T(8,128)} %adj.3) | copy-start | bytes 2359300
  0.0 21.0 %copy-start.2 = (f32[8,64,128]{2,1,0:T(8,128)S(1)}, f32[8,64,128]{2,1,0:T(8,128)}, u32[]{:S(2)}) copy-start(f32[8,64,128]{2,1,0:T(8,128)} %eps.3) | copy-start | bytes 786436
  3.3 10.8 %collective-permute-start = (f32[13,64,128]{2,1,0:T(8,128)}, f32[13,64,128]{2,1,0:T(8,128)S(1)}, u32[]{:S(2)}, u32[]{:S(2)}) collective-permute-start(f32[13,64,128]{2,1,0:T(8,128)} %get-tuple-element.7), channel_id=1, source_target_pairs={{0,1},{1,2},{2,3},{3,4},{4,5},{5,6},{6,7},{7,8},{8,9},{9,10},{10,1... | collective-permute-start | bytes 1277960 | tf_op jit(solution)/shard_map/ppermute | solution.py:238
  7.7 13.3 %collective-permute-start.1 = (f32[13,64,128]{2,1,0:T(8,128)}, f32[13,64,128]{2,1,0:T(8,128)S(1)}, u32[]{:S(2)}, u32[]{:S(2)}) collective-permute-start(f32[13,64,128]{2,1,0:T(8,128)} %get-tuple-element.8), channel_id=1, source_target_pairs={{1,0},{2,1},{3,2},{4,3},{5,4},{6,5},{7,6},{8,7},{9,8},{10,9},{11,1... | collective-permute-start | bytes 1277960 | tf_op jit(solution)/shard_map/ppermute | solution.py:239
  27.4 4.2 %copy-start.4 = (s32[8,8]{1,0:T(8,128)S(1)}, s32[8,8]{1,0:T(8,128)}, u32[]{:S(2)}) copy-start(s32[8,8]{1,0:T(8,128)} %param.9) | copy-start | bytes 772
  27.4 10.2 %all-to-all-start = ((f32[8,64,128]{2,1,0:T(8,128)}), f32[8,64,128]{2,1,0:T(8,128)S(1)}, u32[]{:S(2)}, u32[]{:S(2)}) async-start(f32[8,64,128]{2,1,0:T(8,128)} %bitcast.3), calls=%async_computation | async-start | bytes 524288 | tf_op jit(solution)/shard_map/all_to_all | solution.py:250
  37.6 0.7 %copy-start.3 = (f32[8,64,128]{2,1,0:T(8,128)}, f32[8,64,128]{2,1,0:T(8,128)S(1)}, u32[]{:S(2)}) copy-start(f32[8,64,128]{2,1,0:T(8,128)S(1)} %all-to-all-done.refs_0_) | copy-start | bytes 786436

commit v2 on v1

v2 whole, which is shorter than its diff:
```python
import jax
import jax.numpy as jnp
from jax import lax
from jax.experimental import pallas as pl
from jax.experimental.pallas import tpu as pltpu
from jax.sharding import PartitionSpec as P

ITERS = 4
PIX_DEV = 16
CAP = 4
DEPTH = 3
F32 = jnp.float32
BF16 = jnp.bfloat16
MIB = 1024 * 1024


def add(a, b):
    return b if a is None else a if b is None else a + b


def sub(a, b):
    return a if b is None else -b if a is None else a - b


def mul(a, b):
    return None if a is None or b is None else a * b


def y_ahead(a):
    return None if a is None else pltpu.roll(a, a.shape[0] - 1, 0) - a


def y_behind(a):
    return None if a is None else a - pltpu.roll(a, 1, 0)


def z_ahead(a):
    return None if a is None else pltpu.roll(a, a.shape[1] - 1, 1) - a


def z_behind(a):
    return None if a is None else a - pltpu.roll(a, 1, 1)


def curl_f(v, v2_next, v3_next):
    v1, v2, v3 = v
    z1, z2 = z_ahead(v1), z_ahead(v2)
    h2 = sub(z1, sub(v3_next, v3))
    h1 = sub(y_ahead(v3), z2)
    h3 = sub(sub(v2_next, v2), y_ahead(v1))
    return h1, h2, h3


def scaled_curl_b(h, h2_prev, h3_prev, e):
    h1, h2, h3 = h
    z1, z2 = z_behind(h1), z_behind(h2)
    return (
        mul(e, sub(y_behind(h3), z2)),
        mul(e, sub(z1, sub(h3, h3_prev))),
        mul(e, sub(sub(h2, h2_prev), y_behind(h1))),
    )


E_ROW = 4
SPANS = ((0, 5), (5, 4), (9, 4))


def trace_row(run, k):
    return SPANS[k][0] + 2 * run


def edge_kernel(
    fwd_hbm, adj_hbm, eps_hbm, next_hbm, prev_hbm, current, eps, to_next, to_prev, sem, out_sem
):
    last = eps_hbm.shape[0] - 1
    runs = range(2)
    copies = []
    for at in (0, last + 1 - DEPTH):
        span = pl.ds(at, DEPTH)
        copies.append((eps_hbm.at[span], eps.at[span]))
        for run, whole in enumerate((fwd_hbm, adj_hbm)):
            copies.append((whole.at[0, :, span], current.at[run, :, span]))
    copies = [pltpu.make_async_copy(a, b, sem.at[n]) for n, (a, b) in enumerate(copies)]
    for copy in copies:
        copy.start()
    for copy in copies:
        copy.wait()

    def source(run, i):
        e = -0.25 * eps[i]
        return tuple(e * current[run, c, i] for c in range(3))

    def put_next(run, k, v):
        to_next[trace_row(run, k)] = v[2] + z_ahead(v[0])
        to_next[trace_row(run, k) + 1] = v[1] + y_ahead(v[0])

    def put_prev(run, k, v):
        to_prev[trace_row(run, k)] = v[1]
        to_prev[trace_row(run, k) + 1] = v[2]

    sent = []

    def send(k):
        span = pl.ds(*SPANS[k])
        for n, (a, b) in enumerate(((to_next, next_hbm), (to_prev, prev_hbm))):
            sent.append(pltpu.make_async_copy(a.at[span], b.at[span], out_sem.at[2 * k + n]))
            sent[-1].start()

    end = [[source(r, last - 2), source(r, last - 1), source(r, last)] for r in runs]
    first = [[source(r, 0), source(r, 1), source(r, 2)] for r in runs]
    for r in runs:
        put_next(r, 0, end[r][2])
        put_prev(r, 0, first[r][0])
    to_next[E_ROW] = -0.25 * eps[last]
    to_prev[E_ROW] = -0.25 * eps[0]
    send(0)
    end_h = [
        [curl_f(a, b[1], b[2]), curl_f(b, c[1], c[2]), curl_f(c, None, None)] for a, b, c in end
    ]
    first_h = [[curl_f(a, b[1], b[2]), curl_f(b, c[1], c[2])] for a, b, c in first]
    end1 = [
        [
            scaled_curl_b(hb, ha[1], ha[2], -0.25 * eps[last - 1]),
            scaled_curl_b(hc, hb[1], hb[2], -0.25 * eps[last]),
        ]
        for ha, hb, hc in end_h
    ]
    first1 = [
        [
            scaled_curl_b(ha, -v[0][2], v[0][1], -0.25 * eps[0]),
            scaled_curl_b(hb, ha[1], ha[2], -0.25 * eps[1]),
        ]
        for (ha, hb), v in zip(first_h, first)
    ]
    for r in runs:
        put_next(r, 1, end1[r][1])
        put_prev(r, 1, first1[r][0])
    send(1)
    end_h = [[curl_f(b, c[1], c[2]), curl_f(c, None, None)] for b, c in end1]
    first_h = [curl_f(a, b[1], b[2]) for a, b in first1]
    end2 = [scaled_curl_b(hc, hb[1], hb[2], -0.25 * eps[last]) for hb, hc in end_h]
    first2 = [
        scaled_curl_b(h, -v[0][2], v[0][1], -0.25 * eps[0]) for h, v in zip(first_h, first1)
    ]
    for r in runs:
        put_next(r, 2, end2[r])
        put_prev(r, 2, first2[r])
    send(2)
    for copy in sent:
        copy.wait()


def pair_factors(sig):
    def by_step(s):
        s1, s2, s3, s4 = s
        return (
            (s1,),
            (s1 + s2, s1),
            (s1 + s2 + s3, 3.0 * s1 + s2, s1),
            (s1 + s2 + s3 + s4, 6.0 * s1 + 3.0 * s2 + s3, 5.0 * s1 + s2, s1),
        )

    f = by_step([sig[i] for i in range(ITERS)])
    a = by_step([sig[ITERS + i] for i in range(ITERS)])
    factors = {}
    for t in range(ITERS):
        for k, fk in enumerate(f[t]):
            for m, am in enumerate(a[ITERS - 1 - t]):
                factors[k, m] = factors.get((k, m), 0.0) + 4.0 * fk * am
    return factors


REACHED = tuple((depth, k) for depth in range(DEPTH) for k in range(depth + 1, DEPTH + 1))


def own_kernel(sig, fwd, adj, eps, fp_row, fp_col, out, near, mixes, put, v):
    planes = eps.shape[0]
    last = planes - 1
    has_prev = sig[8]
    factors = pair_factors(sig)

    def start(i, _):
        e = -0.25 * eps[i]
        for run, current in enumerate((fwd, adj)):
            for c in range(3):
                v[0, run, c, i] = e * current[0, c, i]
        return 0

    lax.fori_loop(0, planes, start, 0)

    def read(k, run, i):
        return tuple(v[k, run, c, i] for c in range(3))

    for k in range(DEPTH):
        behind = []
        for run in range(2):
            if k < 2:
                near[run, 2 * k] = v[k, run, 1, 0]
                near[run, 2 * k + 1] = v[k, run, 2, 0]
            behind += [v[k, run, 2, 0] * -has_prev, v[k, run, 1, 0] * has_prev]

        def finish(i, new):
            if k < 2:
                for run in range(2):
                    for c in range(3):
                        v[k + 1, run, c, i] = new[run][c]
                return
            total = None
            for c in range(3):
                f = [v[j, 0, c, i] for j in range(DEPTH)] + [new[0][c]]
                a = [v[j, 1, c, i] for j in range(DEPTH)] + [new[1][c]]
                for m in range(4):
                    mix = None
                    for j in range(4 - m):
                        mix = add(mix, factors[j, m] * f[j])
                    total = add(total, mix * a[m])
            for block in range(out.shape[0]):
                out[block, i] = total[block * 8 : block * 8 + 8]

        def plane(i, carry):
            e = -0.25 * eps[i]
            h = [curl_f(read(k, r, i), v[k, r, 1, i + 1], v[k, r, 2, i + 1]) for r in range(2)]
            finish(i, [scaled_curl_b(h[r], carry[2 * r], carry[2 * r + 1], e) for r in range(2)])
            return h[0][1], h[0][2], h[1][1], h[1][2]

        carry = lax.fori_loop(0, last, plane, tuple(behind))
        new = []
        for run in range(2):
            h = curl_f(read(k, run, last), None, None)
            if k < 2:
                near[run, 4 + 2 * k] = h[1]
                near[run, 5 + 2 * k] = h[2]
            new.append(scaled_curl_b(h, carry[2 * run], carry[2 * run + 1], -0.25 * eps[last]))
        finish(last, new)

    for side in range(2):
        for n, (depth, k) in enumerate(REACHED):
            i = last - depth if side else depth
            for c in range(3):
                for run in range(2):
                    mix = None
                    for j in range(4 - k):
                        factor = factors[(j, k) if run else (k, j)]
                        mix = add(mix, factor * v[j, 1 - run, c, i])
                    mixes[side, run, n, c] = mix

    count = fp_row.shape[1]
    owners = put.shape[0] // (2 * CAP)
    row_owner = (fp_row[...] >> 4) & (owners - 1)
    col_owner = (fp_col[...] >> 4) & (owners - 1)
    earlier = lax.broadcasted_iota(jnp.int32, (count, count), 0) < lax.broadcasted_iota(
        jnp.int32, (count, count), 1
    )
    same = (row_owner == col_owner) & earlier
    rank = jnp.sum(same.astype(F32), axis=0, keepdims=True).astype(jnp.int32)
    slot = row_owner * (2 * CAP) + rank
    rows = lax.broadcasted_iota(jnp.int32, (put.shape[0], count), 0)
    value = (rows == slot).astype(F32)
    mark = (rows == slot + CAP).astype(F32)
    put[...] = jnp.concatenate([value, value, value, mark], axis=1).astype(BF16)


def join_kernel(sig, eps, grad, near, mixes, from_prev, from_next, out):
    last = eps.shape[0] - 1
    has_prev, has_next = sig[8], sig[9]
    runs = range(2)
    e_prev, e_next = from_prev[E_ROW] * has_prev, from_next[E_ROW] * has_next
    e = {i: -0.25 * eps[i] for i in (0, 1, 2, last - 2, last - 1, last)}
    factors = pair_factors(sig)

    def left_trace(r, k):
        row = trace_row(r, k)
        return from_prev[row] * has_prev, from_prev[row + 1] * -has_prev

    def right_trace(r, k):
        row = trace_row(r, k)
        return from_next[row + 1] * -has_next, from_next[row] * has_next

    def passed(h, e):
        return None, e * h[1], -e * h[0]

    t = [left_trace(r, 0) for r in runs]
    u = [right_trace(r, 0) for r in runs]
    own = [(None, -near[r, 1], near[r, 0]) for r in runs]
    c = [scaled_curl_b(own[r], None, None, e_prev) for r in runs]
    g1 = [scaled_curl_b((None, *u[r]), None, None, e[last]) for r in runs]
    f1 = [passed(t[r], e[0]) for r in runs]
    d = [passed((near[r, 4], near[r, 5]), e_next) for r in runs]
    h0 = [curl_f(f1[r], None, None) for r in runs]
    hm = [curl_f(c[r], f1[r][1], f1[r][2]) for r in runs]
    hd = [curl_f(d[r], None, None) for r in runs]
    h7 = [curl_f(g1[r], d[r][1], d[r][2]) for r in runs]
    h6 = [(-g1[r][2], g1[r][1]) for r in runs]
    t = [left_trace(r, 1) for r in runs]
    u = [right_trace(r, 1) for r in runs]
    f2a = [scaled_curl_b(h0[r], hm[r][1] + t[r][0], hm[r][2] + t[r][1], e[0]) for r in runs]
    c = [
        scaled_curl_b(
            (hm[r][0], hm[r][1] - near[r, 3], hm[r][2] + near[r, 2]), -c[r][2], c[r][1], e_prev
        )
        for r in runs
    ]
    f2b = [passed(h0[r][1:], e[1]) for r in runs]
    g2a = [
        scaled_curl_b((h7[r][0], h7[r][1] + u[r][0], h7[r][2] + u[r][1]), *h6[r], e[last])
        for r in runs
    ]
    g2b = [scaled_curl_b((None, *h6[r]), None, None, e[last - 1]) for r in runs]
    d = [
        scaled_curl_b(hd[r], near[r, 6] + h7[r][1], near[r, 7] + h7[r][2], e_next) for r in runs
    ]
    h0 = [curl_f(f2a[r], f2b[r][1], f2b[r][2]) for r in runs]
    h1 = [curl_f(f2b[r], None, None) for r in runs]
    hm = [curl_f(c[r], f2a[r][1], f2a[r][2]) for r in runs]
    h7 = [curl_f(g2a[r], d[r][1], d[r][2]) for r in runs]
    h6 = [curl_f(g2b[r], g2a[r][1], g2a[r][2]) for r in runs]
    h5 = [(-g2b[r][2], g2b[r][1]) for r in runs]
    t = [left_trace(r, 2) for r in runs]
    u = [right_trace(r, 2) for r in runs]
    f3a = [scaled_curl_b(h0[r], hm[r][1] + t[r][0], hm[r][2] + t[r][1], e[0]) for r in runs]
    f3b = [scaled_curl_b(h1[r], h0[r][1], h0[r][2], e[1]) for r in runs]
    f3c = [passed(h1[r][1:], e[2]) for r in runs]
    g3a = [
        scaled_curl_b(
            (h7[r][0], h7[r][1] + u[r][0], h7[r][2] + u[r][1]), h6[r][1], h6[r][2], e[last]
        )
        for r in runs
    ]
    g3b = [scaled_curl_b(h6[r], *h5[r], e[last - 1]) for r in runs]
    g3c = [scaled_curl_b((None, *h5[r]), None, None, e[last - 2]) for r in runs]

    fields = (
        ({(0, 1): f1, (0, 2): f2a, (0, 3): f3a, (1, 2): f2b, (1, 3): f3b, (2, 3): f3c}),
        ({(0, 1): g1, (0, 2): g2a, (0, 3): g3a, (1, 2): g2b, (1, 3): g3b, (2, 3): g3c}),
    )
    for i in range(DEPTH, last + 1 - DEPTH):
        for block in range(out.shape[0]):
            out[block, i] = grad[block, i]
    for side in range(2):
        for depth in range(DEPTH):
            i = last - depth if side else depth
            total = None
            for n, (at, k) in enumerate(REACHED):
                if at == depth:
                    f = fields[side][at, k]
                    for x in range(3):
                        for r in runs:
                            if f[r][x] is not None:
                                total = add(total, f[r][x] * mixes[side, r, n, x])
            if depth == 0:
                one, two = fields[side][0, 1], fields[side][0, 2]
                for x in range(3):
                    if one[0][x] is not None:
                        both = factors[1, 1] * one[1][x] + factors[1, 2] * two[1][x]
                        total = total + one[0][x] * both
                        total = total + two[0][x] * (factors[2, 1] * one[1][x])
            for block in range(out.shape[0]):
                out[block, i] = grad[block, i] + total[block * 8 : block * 8 + 8]


def in_thirds(a):
    high = a.astype(BF16)
    rest = a - high.astype(F32)
    middle = rest.astype(BF16)
    return high, middle, (rest - middle.astype(F32)).astype(BF16)


def pack_kernel(parts, put, fp_col, out):
    count = parts.shape[1]
    summed = parts[0]
    for s in range(1, parts.shape[0]):
        summed = summed + parts[s]
    lanes = lax.broadcasted_iota(jnp.int32, (count, summed.shape[1]), 1)
    pixel = ((fp_col[...] & (PIX_DEV - 1)) == lanes).astype(F32).astype(BF16)
    rows = jnp.concatenate([*in_thirds(summed), pixel], axis=0)
    out[...] = jnp.dot(put[...], rows, preferred_element_type=F32)


def pixel_kernel(arrived, out):
    got = arrived[...]
    rows = lax.broadcasted_iota(jnp.int32, got.shape, 0)
    is_data = (rows & (2 * CAP - 1)) < CAP
    pixel = jnp.where(is_data, pltpu.roll(got, got.shape[0] - CAP, 0), 0.0).astype(BF16)
    sums = None
    for part in in_thirds(got):
        sums = add(
            sums,
            lax.dot_general(pixel, part, (((0,), (0,)), ((), ())), preferred_element_type=F32),
        )
    out[...] = sums[: out.shape[0]]


def per_device(fwd_current, adj_current, inv_eps, wavelength, footprint):
    planes, ny, nz = inv_eps.shape
    space = lax.axis_size("space")
    groups = lax.axis_size("src")
    width = ny // groups
    count = planes * width
    omega = 0.25 + 0.05 * wavelength.astype(F32)
    phases = omega * (jnp.arange(ITERS, dtype=F32) + 1.0)
    here = lax.axis_index("space")
    edges = jnp.stack([here > 0, here < space - 1]).astype(F32)
    sig = jnp.concatenate([jnp.sin(phases), jnp.cos(phases), edges])
    fp_row, fp_col = footprint.reshape(1, count), footprint.reshape(count, 1)

    vmem = pl.BlockSpec(memory_space=pltpu.VMEM)
    smem = pl.BlockSpec(memory_space=pltpu.SMEM)
    hbm = pl.BlockSpec(memory_space=pltpu.HBM)

    def array(*shape, dtype=F32):
        return jax.ShapeDtypeStruct(shape, dtype)

    def call(kernel, outs, mib, args, scratch=(), held=vmem):
        return pl.pallas_call(
            kernel,
            out_shape=outs,
            in_specs=[smem if a is sig else held for a in args],
            out_specs=(held,) * len(outs),
            scratch_shapes=scratch,
            compiler_params=pltpu.CompilerParams(vmem_limit_bytes=mib * MIB),
        )(*args)

    to_next, to_prev = call(
        edge_kernel,
        (array(13, ny, nz), array(13, ny, nz)),
        60,
        (fwd_current, adj_current, inv_eps),
        [
            pltpu.VMEM((2, 3, planes, ny, nz), F32),
            pltpu.VMEM((planes, ny, nz), F32),
            pltpu.VMEM((13, ny, nz), F32),
            pltpu.VMEM((13, ny, nz), F32),
            pltpu.SemaphoreType.DMA((6,)),
            pltpu.SemaphoreType.DMA((6,)),
        ],
        hbm,
    )
    from_prev = lax.ppermute(to_next, "space", [(i, (i + 1) % space) for i in range(space)])
    from_next = lax.ppermute(to_prev, "space", [((i + 1) % space, i) for i in range(space)])
    grad, near, mixes, put = call(
        own_kernel,
        (
            array(groups, planes, width, nz),
            array(2, 8, ny, nz),
            array(2, 2, len(REACHED), 3, ny, nz),
            array(space * 2 * CAP, 4 * count, dtype=BF16),
        ),
        20,
        (sig, fwd_current, adj_current, inv_eps, fp_row, fp_col),
        [
            pltpu.VMEM((3, 2, 3, planes, ny, nz), F32),
        ],
    )
    (grad,) = call(
        join_kernel,
        (array(groups, planes, width, nz),),
        16,
        (sig, inv_eps, grad, near, mixes, from_prev, from_next),
    )
    parts = lax.all_to_all(grad.reshape(groups, count, nz), "src", 0, 0, tiled=True)
    (packed,) = call(pack_kernel, (array(space * 2 * CAP, nz),), 4, (parts, put, fp_col))
    arrived = lax.all_to_all(packed.reshape(space, 2 * CAP, nz), "space", 0, 0, tiled=True)
    (sums,) = call(
        pixel_kernel, (array(PIX_DEV, nz),), 4, (arrived.reshape(space * 2 * CAP, nz),)
    )
    return sums


def solution(mesh):
    in_specs = (
        P("src", None, "space", None, None),
        P("src", None, "space", None, None),
        P("space", None, None),
        P("src"),
        P("space", "src"),
    )
    out_specs = P(("src", "space"), None)
    return jax.shard_map(
        per_device, mesh=mesh, in_specs=in_specs, out_specs=out_specs, check_vma=False
    )
```

time: 64.8 us -> 55.5 us (0.86)
  waiting for transfers between devices: 17.3 us -> 4.36 us
  blocking collectives: 22.3 us -> 31.9 us
  starting transfers between devices: 8.54 us -> 4.46 us
  Pallas kernels: 13.5 us -> 11.2 us
    all_to_all x0 -> x1, blocking collectives: none -> 9.89 us  [per_device(): lax.all_to_all(grad.reshape(groups, count, nz), 'src', 0, 0, tiled=True)]
    ppermute x1, waiting for transfers between devices: 5.57 us -> 0.01 us  [per_device(): lax.ppermute(to_next, 'space', [(i, (i + 1) % space) for i in range(space)])]
    all_to_all x1 -> x0, waiting for transfers between devices: 4.79 us -> none  [per_device(): lax.all_to_all(grad.reshape(groups, count, nz), 'src', 0, 0, tiled=True)]
    all_to_all x1 -> x0, starting transfers between devices: 4.15 us -> none  [per_device(): lax.all_to_all(grad.reshape(groups, count, nz), 'src', 0, 0, tiled=True)]
    ppermute x1, waiting for transfers between devices: 6.9 us -> 4.36 us  [per_device(): lax.ppermute(to_prev, 'space', [((i + 1) % space, i) for i in range(space)])]
    pallas_call x4 -> x5, Pallas kernels: 13.5 us -> 11.2 us  [call(): pl.pallas_call(kernel, out_shape=outs, in_specs=[smem if a is sig else he...]
  transfers between devices with their start and end apart: 3 -> 2, of which waited for: 3 -> 1; matrix products, arithmetic and copies ran while one was open for 2% -> 3% of each run, Pallas kernels for 0% -> 10%
where the time goes in v2:
time: 55.5 us; the launch traced here: 55.3 us
  blocking collectives  31.9 us (57%)
  Pallas kernels  11.2 us (20%)
  starting transfers between devices  4.46 us (8%)
  waiting for transfers between devices  4.36 us (8%)
  local copies, waits for them, and re-layouts  2.48 us (4%)
  between operations  0.71 us (1%)
    all_to_all x1, blocking collectives, per_device(): lax.all_to_all(packed.reshape(space, 2 * CAP, nz), 'space', 0, 0, tiled=T...  22 us
    pallas_call x5, Pallas kernels, call(): pl.pallas_call(kernel, out_shape=outs, in_specs=[smem if a is sig else he...  11.2 us
    all_to_all x1, blocking collectives, per_device(): lax.all_to_all(grad.reshape(groups, count, nz), 'src', 0, 0, tiled=True)  9.89 us
    ppermute x1, starting transfers between devices, per_device(): lax.ppermute(to_next, 'space', [(i, (i + 1) % space) for i in range(space)])  4.46 us
    ppermute x1, waiting for transfers between devices, per_device(): lax.ppermute(to_prev, 'space', [((i + 1) % space, i) for i in range(space)])  4.36 us
    reshape x2, local copies, waits for them, and re-layouts, per_device(): fp_row, fp_col = (footprint.reshape(1, count), footprint.reshape(count, 1))  1.52 us
  transfers between devices with their start and end apart: 2, of which 1 were waited for; matrix products, arithmetic and copies ran while one was open for 3% of the time, Pallas kernels for 10%

profile of v2, /device:TPU:1, one launch (start us, length us, event | category | flops | bytes accessed | tf_op | source)
XLA Modules:
  0.0 55.3 jit_solution(11143357524578599168)
XLA Ops:
  0.0 0.0 copy-start.3
  0.0 0.0 copy-start.1
  0.0 0.0 copy-start
  0.0 2.9 %shard_map.56 = (f32[13,64,128]{2,1,0:T(8,128)}, f32[13,64,128]{2,1,0:T(8,128)}) custom-call(f32[1,3,8,64,128]{4,3,2,1,0:T(8,128)} %fwd_hbm.1, f32[1,3,8,64,128]{4,3,2,1,0:T(8,128)} %adj_hbm.1, f32[8,64,128]{2,1,0:T(8,128)} %eps.3), custom_call_target="tpu_custom_call" | custom-call | tf_op jit(solution)/shard_map/pallas_call | solution.py:414
  2.9 4.5 %collective-permute-start = (f32[13,64,128]{2,1,0:T(8,128)}, f32[13,64,128]{2,1,0:T(8,128)S(1)}, u32[]{:S(2)}, u32[]{:S(2)}) collective-permute-start(f32[13,64,128]{2,1,0:T(8,128)} %get-tuple-element.14), channel_id=1, source_target_pairs={{0,1},{1,2},{2,3},{3,4},{4,5},{5,6},{6,7},{7,8},{8,9},{9,10},{10,1... | collective-permute-start | bytes 1277960 | tf_op jit(solution)/shard_map/ppermute | solution.py:438
  7.4 0.0 collective-permute-start.1
  7.4 0.8 %reshape.15.fp_row = s32[1,64]{1,0:T(1,128)S(1)} reshape(s32[8,8]{1,0:T(8,128)} %param.9) | data formatting | bytes 512 | tf_op jit(solution)/shard_map/reshape | solution.py:404
  8.1 0.8 %reshape.20.fp_col = s32[64,1]{1,0:T(8,128)S(1)} reshape(s32[8,8]{1,0:T(8,128)} %param.9) | data formatting | bytes 512 | tf_op jit(solution)/shard_map/reshape | solution.py:404
  9.5 0.1 add_convert_fusion
  9.7 0.1 pad_maximum_fusion.sig
  9.7 0.0 copy-done.1
  9.7 0.0 copy-done
  9.7 0.0 copy-start.2
  9.8 0.9 %copy-done.2 = f32[8,64,128]{2,1,0:T(8,128)S(1)} copy-done((f32[8,64,128]{2,1,0:T(8,128)S(1)}, f32[8,64,128]{2,1,0:T(8,128)}, u32[]{:S(2)}) %copy-start.2) | copy-done | bytes 262168
  10.7 5.6 %shard_map.55 = (f32[8,8,8,128]{3,2,1,0:T(8,128)S(1)}, f32[2,8,64,128]{3,2,1,0:T(8,128)S(1)}, f32[2,2,6,3,64,128]{5,4,3,2,1,0:T(8,128)S(1)}, bf16[256,256]{1,0:T(8,128)(2,1)S(1)}) custom-call(f32[10]{0:T(128)S(1)} %pad_maximum_fusion.sig, f32[1,3,8,64,128]{4,3,2,1,0:T(8,128)S(1)} %copy-done, f32[1,3,8,64,128]{4,3,2,1,0:T(8,128)S(1)} %copy-done.1, ...), custom_call_target="tpu_custom_call" | custom-call | tf_op jit(solution)/shard_map/pallas_call | solution.py:414
  16.3 0.0 collective-permute-done.from_prev
  16.3 4.4 %collective-permute-done.1.from_next = f32[13,64,128]{2,1,0:T(8,128)S(1)} collective-permute-done((f32[13,64,128]{2,1,0:T(8,128)}, f32[13,64,128]{2,1,0:T(8,128)S(1)}, u32[]{:S(2)}, u32[]{:S(2)}) %collective-permute-start.1) | collective-permute-done | bytes 426016 | tf_op jit(solution)/shard_map/ppermute | solution.py:439
  20.7 0.0 copy-done.3
  20.7 1.7 %shard_map.57 = f32[8,8,8,128]{3,2,1,0:T(8,128)S(1)} custom-call(f32[10]{0:T(128)S(1)} %pad_maximum_fusion.sig, f32[8,64,128]{2,1,0:T(8,128)S(1)} %copy-done.3, f32[8,8,8,128]{3,2,1,0:T(8,128)S(1)} %get-tuple-element.11.grad, f32[2,8,64,128]{3,2,1,0:T(8,128)S(1)} %get-tuple-element.12.near, f32[2,2,6,3,64,128]{5,4,3,2,1,0:T(8,128)S(1)} %get-tuple-element.13.mixes, ...), custom_call_target="tpu_custom_call" | custom-call | tf_op jit(solution)/shard_map/pallas_call | solution.py:414
  22.3 9.9 %all_to_all.10.parts = f32[8,64,128]{2,1,0:T(8,128)S(1)} all-to-all(f32[8,64,128]{2,1,0:T(8,128)S(1)} %bitcast.6), channel_id=1, replica_groups=mesh['src'=8,'space'=32] {'src'}, dimensions={0} | all-to-all | bytes 524288 | tf_op jit(solution)/shard_map/all_to_all | solution.py:460
  32.2 0.2 shard_map.58
  32.5 22.0 %all_to_all.11 = f32[32,8,128]{2,1,0:T(8,128)S(1)} all-to-all(f32[32,8,128]{2,1,0:T(8,128)S(1)} %bitcast.7), channel_id=1, replica_groups=mesh['src'=8,'space'=32] {'space'}, dimensions={0} | all-to-all | bytes 262144 | tf_op jit(solution)/shard_map/all_to_all | solution.py:462
  54.4 0.8 %shard_map.59 = f32[16,128]{1,0:T(8,128)} custom-call(f32[256,128]{1,0:T(8,128)S(1)} %bitcast.8), custom_call_target="tpu_custom_call" | custom-call | tf_op jit(solution)/shard_map/pallas_call | solution.py:414
  (1 shorter events, 0.0 us)
Async XLA Ops:
  0.0 20.7 %copy-start.3 = (f32[8,64,128]{2,1,0:T(8,128)S(1)}, f32[8,64,128]{2,1,0:T(8,128)}, u32[]{:S(2)}) copy-start(f32[8,64,128]{2,1,0:T(8,128)} %eps.3) | copy-start | bytes 786436
  0.0 9.7 %copy-start.1 = (f32[1,3,8,64,128]{4,3,2,1,0:T(8,128)S(1)}, f32[1,3,8,64,128]{4,3,2,1,0:T(8,128)}, u32[]{:S(2)}) copy-start(f32[1,3,8,64,128]{4,3,2,1,0:T(8,128)} %adj_hbm.1) | copy-start | bytes 2359300
  0.0 9.7 %copy-start = (f32[1,3,8,64,128]{4,3,2,1,0:T(8,128)S(1)}, f32[1,3,8,64,128]{4,3,2,1,0:T(8,128)}, u32[]{:S(2)}) copy-start(f32[1,3,8,64,128]{4,3,2,1,0:T(8,128)} %fwd_hbm.1) | copy-start | bytes 2359300
  2.9 13.4 %collective-permute-start = (f32[13,64,128]{2,1,0:T(8,128)}, f32[13,64,128]{2,1,0:T(8,128)S(1)}, u32[]{:S(2)}, u32[]{:S(2)}) collective-permute-start(f32[13,64,128]{2,1,0:T(8,128)} %get-tuple-element.14), channel_id=1, source_target_pairs={{0,1},{1,2},{2,3},{3,4},{4,5},{5,6},{6,7},{7,8},{8,9},{9,10},{10,1... | collective-permute-start | bytes 1277960 | tf_op jit(solution)/shard_map/ppermute | solution.py:438
  7.4 13.3 %collective-permute-start.1 = (f32[13,64,128]{2,1,0:T(8,128)}, f32[13,64,128]{2,1,0:T(8,128)S(1)}, u32[]{:S(2)}, u32[]{:S(2)}) collective-permute-start(f32[13,64,128]{2,1,0:T(8,128)} %get-tuple-element.15), channel_id=1, source_target_pairs={{1,0},{2,1},{3,2},{4,3},{5,4},{6,5},{7,6},{8,7},{9,8},{10,9},{11,1... | collective-permute-start | bytes 1277960 | tf_op jit(solution)/shard_map/ppermute | solution.py:439
  9.7 1.0 %copy-start.2 = (f32[8,64,128]{2,1,0:T(8,128)S(1)}, f32[8,64,128]{2,1,0:T(8,128)}, u32[]{:S(2)}) copy-start(f32[8,64,128]{2,1,0:T(8,128)} %eps.3) | copy-start | bytes 786436

commit v3 on v2

--- a/solution.py
+++ b/solution.py
@@ -1,3 +1,5 @@
+import functools
+
 import jax
 import jax.numpy as jnp
 from jax import lax
@@ -61,93 +63,74 @@
     )
 
 
-E_ROW = 4
-SPANS = ((0, 5), (5, 4), (9, 4))
+E_ROW = 12
 
 
 def trace_row(run, k):
-    return SPANS[k][0] + 2 * run
-
-
-def edge_kernel(
-    fwd_hbm, adj_hbm, eps_hbm, next_hbm, prev_hbm, current, eps, to_next, to_prev, sem, out_sem
-):
-    last = eps_hbm.shape[0] - 1
-    runs = range(2)
-    copies = []
-    for at in (0, last + 1 - DEPTH):
-        span = pl.ds(at, DEPTH)
-        copies.append((eps_hbm.at[span], eps.at[span]))
-        for run, whole in enumerate((fwd_hbm, adj_hbm)):
-            copies.append((whole.at[0, :, span], current.at[run, :, span]))
+    return 6 * run + 2 * k
+
+
+def next_is_partner(on_chip):
+    return (lax.axis_index("space") % 2 == 0) == on_chip
+
+
+def edge_kernel(on_chip, fwd_hbm, adj_hbm, eps_hbm, traces, current, eps, sem):
+    to_next = next_is_partner(on_chip)
+    span = pl.ds(jnp.where(to_next, eps_hbm.shape[0] - DEPTH, 0), DEPTH)
+    copies = [(eps_hbm.at[span], eps)]
+    for run, whole in enumerate((fwd_hbm, adj_hbm)):
+        copies.append((whole.at[0, :, span], current.at[run]))
     copies = [pltpu.make_async_copy(a, b, sem.at[n]) for n, (a, b) in enumerate(copies)]
     for copy in copies:
         copy.start()
     for copy in copies:
         copy.wait()
 
-    def source(run, i):
-        e = -0.25 * eps[i]
-        return tuple(e * current[run, c, i] for c in range(3))
-
-    def put_next(run, k, v):
-        to_next[trace_row(run, k)] = v[2] + z_ahead(v[0])
-        to_next[trace_row(run, k) + 1] = v[1] + y_ahead(v[0])
-
-    def put_prev(run, k, v):
-        to_prev[trace_row(run, k)] = v[1]
-        to_prev[trace_row(run, k) + 1] = v[2]
-
-    sent = []
-
-    def send(k):
-        span = pl.ds(*SPANS[k])
-        for n, (a, b) in enumerate(((to_next, next_hbm), (to_prev, prev_hbm))):
-            sent.append(pltpu.make_async_copy(a.at[span], b.at[span], out_sem.at[2 * k + n]))
-            sent[-1].start()
-
-    end = [[source(r, last - 2), source(r, last - 1), source(r, last)] for r in runs]
-    first = [[source(r, 0), source(r, 1), source(r, 2)] for r in runs]
-    for r in runs:
-        put_next(r, 0, end[r][2])
-        put_prev(r, 0, first[r][0])
-    to_next[E_ROW] = -0.25 * eps[last]
-    to_prev[E_ROW] = -0.25 * eps[0]
-    send(0)
-    end_h = [
-        [curl_f(a, b[1], b[2]), curl_f(b, c[1], c[2]), curl_f(c, None, None)] for a, b, c in end
-    ]
-    first_h = [[curl_f(a, b[1], b[2]), curl_f(b, c[1], c[2])] for a, b, c in first]
-    end1 = [
-        [
-            scaled_curl_b(hb, ha[1], ha[2], -0.25 * eps[last - 1]),
-            scaled_curl_b(hc, hb[1], hb[2], -0.25 * eps[last]),
+    def sources():
+        e = [-0.25 * eps[i] for i in range(DEPTH)]
+        v = [
+            [tuple(e[i] * current[run, c, i] for c in range(3)) for i in range(DEPTH)]
+            for run in range(2)
         ]
-        for ha, hb, hc in end_h
-    ]
-    first1 = [
-        [
-            scaled_curl_b(ha, -v[0][2], v[0][1], -0.25 * eps[0]),
-            scaled_curl_b(hb, ha[1], ha[2], -0.25 * eps[1]),
+        return e, v
+
+    @pl.when(to_next)
+    def _():
+        def put(k, plane):
+            for run, v in enumerate(plane):
+                traces[trace_row(run, k)] = v[2] + z_ahead(v[0])
+                traces[trace_row(run, k) + 1] = v[1] + y_ahead(v[0])
+
+        e, v = sources()
+        traces[E_ROW] = e[2]
+        put(0, [c for _, _, c in v])
+        h = [(curl_f(a, b[1], b[2]), curl_f(b, c[1], c[2]), curl_f(c, None, None)) for a, b, c in v]
+        v = [
+            (scaled_curl_b(hb, ha[1], ha[2], e[1]), scaled_curl_b(hc, hb[1], hb[2], e[2]))
+            for ha, hb, hc in h
         ]
-        for (ha, hb), v in zip(first_h, first)
-    ]
-    for r in runs:
-        put_next(r, 1, end1[r][1])
-        put_prev(r, 1, first1[r][0])
-    send(1)
-    end_h = [[curl_f(b, c[1], c[2]), curl_f(c, None, None)] for b, c in end1]
-    first_h = [curl_f(a, b[1], b[2]) for a, b in first1]
-    end2 = [scaled_curl_b(hc, hb[1], hb[2], -0.25 * eps[last]) for hb, hc in end_h]
-    first2 = [
-        scaled_curl_b(h, -v[0][2], v[0][1], -0.25 * eps[0]) for h, v in zip(first_h, first1)
-    ]
-    for r in runs:
-        put_next(r, 2, end2[r])
-        put_prev(r, 2, first2[r])
-    send(2)
-    for copy in sent:
-        copy.wait()
+        put(1, [c for _, c in v])
+        h = [(curl_f(b, c[1], c[2]), curl_f(c, None, None)) for b, c in v]
+        put(2, [scaled_curl_b(hc, hb[1], hb[2], e[2]) for hb, hc in h])
+
+    @pl.when(jnp.logical_not(to_next))
+    def _():
+        def put(k, plane):
+            for run, v in enumerate(plane):
+                traces[trace_row(run, k)] = v[1]
+                traces[trace_row(run, k) + 1] = v[2]
+
+        e, v = sources()
+        traces[E_ROW] = e[0]
+        put(0, [a for a, _, _ in v])
+        h = [(curl_f(a, b[1], b[2]), curl_f(b, c[1], c[2])) for a, b, c in v]
+        v = [
+            (scaled_curl_b(ha, -a[2], a[1], e[0]), scaled_curl_b(hb, ha[1], ha[2], e[1]))
+            for (ha, hb), (a, _, _) in zip(h, v)
+        ]
+        put(1, [a for a, _ in v])
+        h = [curl_f(a, b[1], b[2]) for a, b in v]
+        put(2, [scaled_curl_b(ha, -a[2], a[1], e[0]) for ha, (a, _) in zip(h, v)])
 
 
 def pair_factors(sig):
@@ -173,7 +156,15 @@
 REACHED = tuple((depth, k) for depth in range(DEPTH) for k in range(depth + 1, DEPTH + 1))
 
 
-def own_kernel(sig, fwd, adj, eps, fp_row, fp_col, out, near, mixes, put, v):
+def own_kernel(
+    sig, fwd_hbm, adj_hbm, eps_hbm, footprint, out, near, mixes, put, pixel, v, fwd, adj, eps, sem
+):
+    pairs = ((fwd_hbm, fwd), (adj_hbm, adj), (eps_hbm, eps))
+    copies = [pltpu.make_async_copy(a, b, sem.at[n]) for n, (a, b) in enumerate(pairs)]
+    for copy in copies:
+        copy.start()
+    for copy in copies:
+        copy.wait()
     planes = eps.shape[0]
     last = planes - 1
     has_prev = sig[8]
@@ -244,10 +235,25 @@
                         mix = add(mix, factor * v[j, 1 - run, c, i])
                     mixes[side, run, n, c] = mix
 
-    count = fp_row.shape[1]
+    wide, width = footprint.shape
+    count = wide * width
     owners = put.shape[0] // (2 * CAP)
-    row_owner = (fp_row[...] >> 4) & (owners - 1)
-    col_owner = (fp_col[...] >> 4) & (owners - 1)
+    ids = footprint[...]
+    by_row = jnp.concatenate(
+        [jnp.broadcast_to(ids[i : i + 1], (width, width)) for i in range(wide)], axis=0
+    ).astype(F32)
+    at = lax.broadcasted_iota(jnp.int32, (count, width), 0) % width
+    own = at == lax.broadcasted_iota(jnp.int32, (count, width), 1)
+    col = jnp.sum(jnp.where(own, by_row, 0.0), axis=1, keepdims=True)
+    diagonal = lax.broadcasted_iota(jnp.int32, (count, count), 0) == lax.broadcasted_iota(
+        jnp.int32, (count, count), 1
+    )
+    row = jnp.sum(jnp.where(diagonal, col, 0.0), axis=0, keepdims=True)
+    row, col = row.astype(jnp.int32), col.astype(jnp.int32)
+    lanes = lax.broadcasted_iota(jnp.int32, pixel.shape, 1)
+    pixel[...] = ((col & (PIX_DEV - 1)) == lanes).astype(F32).astype(BF16)
+    row_owner = (row >> 4) & (owners - 1)
+    col_owner = (col >> 4) & (owners - 1)
     earlier = lax.broadcasted_iota(jnp.int32, (count, count), 0) < lax.broadcasted_iota(
         jnp.int32, (count, count), 1
     )
@@ -260,21 +266,29 @@
     put[...] = jnp.concatenate([value, value, value, mark], axis=1).astype(BF16)
 
 
-def join_kernel(sig, eps, grad, near, mixes, from_prev, from_next, out):
+def join_kernel(sig, eps, grad, near, mixes, from_ring, from_chip, out):
     last = eps.shape[0] - 1
     has_prev, has_next = sig[8], sig[9]
     runs = range(2)
-    e_prev, e_next = from_prev[E_ROW] * has_prev, from_next[E_ROW] * has_next
+    first_of_pair = lax.axis_index("space") % 2 == 0
+
+    def from_prev(row):
+        return jnp.where(first_of_pair, from_ring[row], from_chip[row])
+
+    def from_next(row):
+        return jnp.where(first_of_pair, from_chip[row], from_ring[row])
+
+    e_prev, e_next = from_prev(E_ROW) * has_prev, from_next(E_ROW) * has_next
     e = {i: -0.25 * eps[i] for i in (0, 1, 2, last - 2, last - 1, last)}
     factors = pair_factors(sig)
 
     def left_trace(r, k):
         row = trace_row(r, k)
-        return from_prev[row] * has_prev, from_prev[row + 1] * -has_prev
+        return from_prev(row) * has_prev, from_prev(row + 1) * -has_prev
 
     def right_trace(r, k):
         row = trace_row(r, k)
-        return from_next[row + 1] * -has_next, from_next[row] * has_next
+        return from_next(row + 1) * -has_next, from_next(row) * has_next
 
     def passed(h, e):
         return None, e * h[1], -e * h[0]
@@ -365,14 +379,11 @@
     return high, middle, (rest - middle.astype(F32)).astype(BF16)
 
 
-def pack_kernel(parts, put, fp_col, out):
-    count = parts.shape[1]
+def pack_kernel(parts, put, pixel, out):
     summed = parts[0]
     for s in range(1, parts.shape[0]):
         summed = summed + parts[s]
-    lanes = lax.broadcasted_iota(jnp.int32, (count, summed.shape[1]), 1)
-    pixel = ((fp_col[...] & (PIX_DEV - 1)) == lanes).astype(F32).astype(BF16)
-    rows = jnp.concatenate([*in_thirds(summed), pixel], axis=0)
+    rows = jnp.concatenate([*in_thirds(summed), pixel[...]], axis=0)
     out[...] = jnp.dot(put[...], rows, preferred_element_type=F32)
 
 
@@ -401,7 +412,6 @@
     here = lax.axis_index("space")
     edges = jnp.stack([here > 0, here < space - 1]).astype(F32)
     sig = jnp.concatenate([jnp.sin(phases), jnp.cos(phases), edges])
-    fp_row, fp_col = footprint.reshape(1, count), footprint.reshape(count, 1)
 
     vmem = pl.BlockSpec(memory_space=pltpu.VMEM)
     smem = pl.BlockSpec(memory_space=pltpu.SMEM)
@@ -410,55 +420,71 @@
     def array(*shape, dtype=F32):
         return jax.ShapeDtypeStruct(shape, dtype)
 
-    def call(kernel, outs, mib, args, scratch=(), held=vmem):
+    held = [
+        pltpu.with_memory_space_constraint(a, pltpu.HBM)
+        for a in (fwd_current, adj_current, inv_eps)
+    ]
+
+    def call(kernel, outs, mib, args, scratch=(), aliases=()):
         return pl.pallas_call(
             kernel,
             out_shape=outs,
-            in_specs=[smem if a is sig else held for a in args],
-            out_specs=(held,) * len(outs),
+            in_specs=[
+                smem if a is sig else hbm if any(a is b for b in held) else vmem for a in args
+            ],
+            out_specs=(vmem,) * len(outs),
             scratch_shapes=scratch,
+            input_output_aliases=dict(aliases),
             compiler_params=pltpu.CompilerParams(vmem_limit_bytes=mib * MIB),
         )(*args)
 
-    to_next, to_prev = call(
-        edge_kernel,
-        (array(13, ny, nz), array(13, ny, nz)),
-        60,
-        (fwd_current, adj_current, inv_eps),
-        [
-            pltpu.VMEM((2, 3, planes, ny, nz), F32),
-            pltpu.VMEM((planes, ny, nz), F32),
-            pltpu.VMEM((13, ny, nz), F32),
-            pltpu.VMEM((13, ny, nz), F32),
-            pltpu.SemaphoreType.DMA((6,)),
-            pltpu.SemaphoreType.DMA((6,)),
-        ],
-        hbm,
-    )
-    from_prev = lax.ppermute(to_next, "space", [(i, (i + 1) % space) for i in range(space)])
-    from_next = lax.ppermute(to_prev, "space", [((i + 1) % space, i) for i in range(space)])
-    grad, near, mixes, put = call(
+    def traces_for(on_chip):
+        (traces,) = call(
+            functools.partial(edge_kernel, on_chip),
+            (array(E_ROW + 1, ny, nz),),
+            4,
+            held,
+            [
+                pltpu.VMEM((2, 3, DEPTH, ny, nz), F32),
+                pltpu.VMEM((DEPTH, ny, nz), F32),
+                pltpu.SemaphoreType.DMA((3,)),
+            ],
+        )
+        return traces
+
+    from_chip = lax.ppermute(traces_for(True), "space", [(i, i ^ 1) for i in range(space)])
+    from_ring = lax.ppermute(
+        traces_for(False),
+        "space",
+        [(i, min(max(i - 1 if i % 2 == 0 else i + 1, 0), space - 1)) for i in range(space)],
+    )
+    grad, near, mixes, put, pixel = call(
         own_kernel,
         (
             array(groups, planes, width, nz),
             array(2, 8, ny, nz),
             array(2, 2, len(REACHED), 3, ny, nz),
             array(space * 2 * CAP, 4 * count, dtype=BF16),
+            array(count, nz, dtype=BF16),
         ),
         20,
-        (sig, fwd_current, adj_current, inv_eps, fp_row, fp_col),
+        (sig, *held, footprint),
         [
             pltpu.VMEM((3, 2, 3, planes, ny, nz), F32),
+            pltpu.VMEM(fwd_current.shape, F32),
+            pltpu.VMEM(fwd_current.shape, F32),
+            pltpu.VMEM((planes, ny, nz), F32),
+            pltpu.SemaphoreType.DMA((3,)),
         ],
     )
     (grad,) = call(
         join_kernel,
         (array(groups, planes, width, nz),),
         16,
-        (sig, inv_eps, grad, near, mixes, from_prev, from_next),
+        (sig, inv_eps, grad, near, mixes, from_ring, from_chip),
     )
     parts = lax.all_to_all(grad.reshape(groups, count, nz), "src", 0, 0, tiled=True)
-    (packed,) = call(pack_kernel, (array(space * 2 * CAP, nz),), 4, (parts, put, fp_col))
+    (packed,) = call(pack_kernel, (array(space * 2 * CAP, nz),), 4, (parts, put, pixel))
     arrived = lax.all_to_all(packed.reshape(space, 2 * CAP, nz), "space", 0, 0, tiled=True)
     (sums,) = call(
         pixel_kernel, (array(PIX_DEV, nz),), 4, (arrived.reshape(space * 2 * CAP, nz),)

time: 55.5 us -> 55.1 us (level)
  waiting for transfers between devices: 4.36 us -> 0.89 us
  local copies, waits for them, and re-layouts: 2.48 us -> 0.01 us
  starting transfers between devices: 4.46 us -> 6.42 us
  blocking collectives: 31.9 us -> 33.8 us
  Pallas kernels: 11.2 us -> 12.8 us
    ppermute x2, waiting for transfers between devices: 4.36 us -> 0.89 us  [the longest x1 0.89 us: per_device(): lax.ppermute(traces_for(False), 'space', [(i, min(max(i - 1 if i % 2 == 0...]
    ppermute x2, starting transfers between devices: 4.46 us -> 6.42 us  [the longest x1 6.32 us: per_device(): lax.ppermute(traces_for(False), 'space', [(i, min(max(i - 1 if i % 2 == 0...]
    pallas_call x5 -> x6, Pallas kernels: 11.2 us -> 12.8 us  [call(): pl.pallas_call(kernel, out_shape=outs, in_specs=[smem if a is sig else hb...]
    reshape x2 -> x0, local copies, waits for them, and re-layouts: 1.52 us -> none  [per_device(): fp_row, fp_col = (footprint.reshape(1, count), footprint.reshape(count, 1))]
    all_to_all x1, blocking collectives: 22 us -> 23.3 us  [per_device(): lax.all_to_all(packed.reshape(space, 2 * CAP, nz), 'space', 0, 0, tiled=T...]
    unnamed x8 -> x4, local copies, waits for them, and re-layouts: 0.96 us -> 0.01 us
    all_to_all x1, blocking collectives: 9.89 us -> 10.5 us  [per_device(): lax.all_to_all(grad.reshape(groups, count, nz), 'src', 0, 0, tiled=True)]
  transfers between devices with their start and end apart: 2 -> 2, of which waited for: 1 -> 1; matrix products, arithmetic and copies ran while one was open for 3% -> 0% of each run, Pallas kernels for 10% -> 16%
where the time goes in v3:
time: 55.1 us; the launch traced here: 54.8 us
  blocking collectives  33.8 us (61%)
  Pallas kernels  12.8 us (23%)
  starting transfers between devices  6.42 us (12%)
  waiting for transfers between devices  0.89 us (2%)
  between operations  0.72 us (1%)
    all_to_all x1, blocking collectives, per_device(): lax.all_to_all(packed.reshape(space, 2 * CAP, nz), 'space', 0, 0, tiled=T...  23.3 us
    pallas_call x6, Pallas kernels, call(): pl.pallas_call(kernel, out_shape=outs, in_specs=[smem if a is sig else hb...  12.8 us
    all_to_all x1, blocking collectives, per_device(): lax.all_to_all(grad.reshape(groups, count, nz), 'src', 0, 0, tiled=True)  10.5 us
    ppermute x1, starting transfers between devices, per_device(): lax.ppermute(traces_for(False), 'space', [(i, min(max(i - 1 if i % 2 == 0...  6.32 us
  transfers between devices with their start and end apart: 2, of which 1 were waited for; matrix products, arithmetic and copies ran while one was open for 0% of the time, Pallas kernels for 16%

profile of v3, /device:TPU:1, one launch (start us, length us, event | category | flops | bytes accessed | tf_op | source)
XLA Modules:
  0.0 54.8 jit_solution(17458855815801617465)
XLA Ops:
  0.0 0.0 copy-start.1
  0.0 1.6 %shard_map.56 = f32[13,64,128]{2,1,0:T(8,128)S(1)} custom-call(f32[1,3,8,64,128]{4,3,2,1,0:T(8,128)} %fwd_hbm.5, f32[1,3,8,64,128]{4,3,2,1,0:T(8,128)} %adj_hbm.5, f32[8,64,128]{2,1,0:T(8,128)} %eps.1), custom_call_target="tpu_custom_call" | custom-call | tf_op jit(solution)/shard_map/pallas_call | solution.py:429
  1.6 0.0 copy-start
  1.6 6.3 %collective-permute-start = (f32[13,64,128]{2,1,0:T(8,128)S(1)}, f32[13,64,128]{2,1,0:T(8,128)S(1)}, u32[]{:S(2)}, u32[]{:S(2)}) collective-permute-start(f32[13,64,128]{2,1,0:T(8,128)S(1)} %shard_map.56), channel_id=1, source_target_pairs={{0,0},{1,2},{2,1},{3,4},{4,3},{5,6},{6,5},{7,8},{8,7},{9,10},{10,9... | collective-permute-start | bytes 1277960 | tf_op jit(solution)/shard_map/ppermute | solution.py:456
  7.9 1.5 %shard_map.57 = f32[13,64,128]{2,1,0:T(8,128)S(1)} custom-call(f32[1,3,8,64,128]{4,3,2,1,0:T(8,128)} %fwd_hbm.5, f32[1,3,8,64,128]{4,3,2,1,0:T(8,128)} %adj_hbm.5, f32[8,64,128]{2,1,0:T(8,128)} %eps.1), custom_call_target="tpu_custom_call" | custom-call | tf_op jit(solution)/shard_map/pallas_call | solution.py:429
  9.4 0.1 collective-permute-start.1
  10.2 0.1 add_convert_fusion
  10.3 0.1 pad_maximum_fusion.sig
  10.4 0.0 copy-done.1
  10.4 7.0 %shard_map.55 = (f32[8,8,8,128]{3,2,1,0:T(8,128)S(1)}, f32[2,8,64,128]{3,2,1,0:T(8,128)S(1)}, f32[2,2,6,3,64,128]{5,4,3,2,1,0:T(8,128)S(1)}, bf16[256,256]{1,0:T(8,128)(2,1)S(1)}, bf16[64,128]{1,0:T(8,128)(2,1)S(1)}) custom-call(f32[10]{0:T(128)S(1)} %pad_maximum_fusion.sig, f32[1,3,8,64,128]{4,3,2,1,0:T(8,128)} %fwd_hbm.5, f32[1,3,8,64,128]{4,3,2,1,0:T(8,128)} %adj_hbm.5, ...), custom_call_target="tpu_custom_call" | custom-call | tf_op jit(solution)/shard_map/pallas_call | solution.py:429
  17.4 0.9 %collective-permute-done.from_ring = f32[13,64,128]{2,1,0:T(8,128)S(1)} collective-permute-done((f32[13,64,128]{2,1,0:T(8,128)S(1)}, f32[13,64,128]{2,1,0:T(8,128)S(1)}, u32[]{:S(2)}, u32[]{:S(2)}) %collective-permute-start) | collective-permute-done | bytes 426016 | tf_op jit(solution)/shard_map/ppermute | solution.py:456
  18.3 0.0 collective-permute-done.1.from_chip
  18.3 0.0 copy-done
  18.3 1.7 %shard_map.58 = f32[8,8,8,128]{3,2,1,0:T(8,128)S(1)} custom-call(f32[10]{0:T(128)S(1)} %pad_maximum_fusion.sig, f32[8,64,128]{2,1,0:T(8,128)S(1)} %copy-done, f32[8,8,8,128]{3,2,1,0:T(8,128)S(1)} %get-tuple-element.10.grad, f32[2,8,64,128]{3,2,1,0:T(8,128)S(1)} %get-tuple-element.11.near, f32[2,2,6,3,64,128]{5,4,3,2,1,0:T(8,128)S(1)} %get-tuple-element.12.mixes, ...), custom_call_target="tpu_custom_call" | custom-call | tf_op jit(solution)/shard_map/pallas_call | solution.py:429
  20.0 10.5 %all_to_all.10.parts = f32[8,64,128]{2,1,0:T(8,128)S(1)} all-to-all(f32[8,64,128]{2,1,0:T(8,128)S(1)} %bitcast.6), channel_id=1, replica_groups=mesh['src'=8,'space'=32] {'src'}, dimensions={0} | all-to-all | bytes 524288 | tf_op jit(solution)/shard_map/all_to_all | solution.py:486
  30.5 0.2 shard_map.59
  30.7 23.3 %all_to_all.11 = f32[32,8,128]{2,1,0:T(8,128)S(1)} all-to-all(f32[32,8,128]{2,1,0:T(8,128)S(1)} %bitcast.8), channel_id=1, replica_groups=mesh['src'=8,'space'=32] {'space'}, dimensions={0} | all-to-all | bytes 262144 | tf_op jit(solution)/shard_map/all_to_all | solution.py:488
  54.0 0.8 %shard_map.60 = f32[16,128]{1,0:T(8,128)} custom-call(f32[256,128]{1,0:T(8,128)S(1)} %bitcast.7), custom_call_target="tpu_custom_call" | custom-call | tf_op jit(solution)/shard_map/pallas_call | solution.py:429
  (1 shorter events, 0.0 us)
Async XLA Ops:
  0.0 10.4 %copy-start.1 = (s32[8,8]{1,0:T(8,128)S(1)}, s32[8,8]{1,0:T(8,128)}, u32[]{:S(2)}) copy-start(s32[8,8]{1,0:T(8,128)} %footprint.1) | copy-start | bytes 772
  1.6 16.7 %copy-start = (f32[8,64,128]{2,1,0:T(8,128)S(1)}, f32[8,64,128]{2,1,0:T(8,128)}, u32[]{:S(2)}) copy-start(f32[8,64,128]{2,1,0:T(8,128)} %eps.1) | copy-start | bytes 786436
  1.6 16.7 %collective-permute-start = (f32[13,64,128]{2,1,0:T(8,128)S(1)}, f32[13,64,128]{2,1,0:T(8,128)S(1)}, u32[]{:S(2)}, u32[]{:S(2)}) collective-permute-start(f32[13,64,128]{2,1,0:T(8,128)S(1)} %shard_map.56), channel_id=1, source_target_pairs={{0,0},{1,2},{2,1},{3,4},{4,3},{5,6},{6,5},{7,8},{8,7},{9,10},{10,9... | collective-permute-start | bytes 1277960 | tf_op jit(solution)/shard_map/ppermute | solution.py:456
  9.4 8.9 %collective-permute-start.1 = (f32[13,64,128]{2,1,0:T(8,128)S(1)}, f32[13,64,128]{2,1,0:T(8,128)S(1)}, u32[]{:S(2)}, u32[]{:S(2)}) collective-permute-start(f32[13,64,128]{2,1,0:T(8,128)S(1)} %shard_map.57), channel_id=1, source_target_pairs={{0,1},{1,0},{2,3},{3,2},{4,5},{5,4},{6,7},{7,6},{8,9},{9,8},{10,11... | collective-permute-start | bytes 1277960 | tf_op jit(solution)/shard_map/ppermute | solution.py:455

commit v4 on v3

--- a/solution.py
+++ b/solution.py
@@ -456,7 +456,7 @@
     from_ring = lax.ppermute(
         traces_for(False),
         "space",
-        [(i, min(max(i - 1 if i % 2 == 0 else i + 1, 0), space - 1)) for i in range(space)],
+        [(i, (i - 1 if i % 2 == 0 else i + 1) % space) for i in range(space)],
     )
     grad, near, mixes, put, pixel = call(
         own_kernel,

time: 55.1 us -> 53.2 us (0.966)
  blocking collectives: 33.8 us -> 29.3 us
  starting transfers between devices: 6.42 us -> 9.97 us
  waiting for transfers between devices: 0.89 us -> 0.01 us
    ppermute x1, starting transfers between devices: 0.09 us -> 5.6 us  [per_device(): lax.ppermute(traces_for(True), 'space', [(i, i ^ 1) for i in range(space)])]
    all_to_all x1, blocking collectives: 23.3 us -> 18.9 us  [per_device(): lax.all_to_all(packed.reshape(space, 2 * CAP, nz), 'space', 0, 0, tiled=T...]
    ppermute x1, starting transfers between devices: 6.32 us -> 4.37 us  [per_device(): lax.ppermute(traces_for(False), 'space', [(i, (i - 1 if i % 2 == 0 else i...]
    ppermute x1, waiting for transfers between devices: 0.89 us -> 0.01 us  [per_device(): lax.ppermute(traces_for(False), 'space', [(i, (i - 1 if i % 2 == 0 else i...]
  transfers between devices with their start and end apart: 2 -> 2, of which waited for: 1 -> 0; matrix products, arithmetic and copies ran while one was open for 0% -> 0% of each run, Pallas kernels for 16% -> 16%
where the time goes in v4:
time: 53.2 us; the launch traced here: 53 us
  blocking collectives  29.3 us (55%)
  Pallas kernels  12.7 us (24%)
  starting transfers between devices  9.97 us (19%)
  between operations  0.73 us (1%)
    all_to_all x1, blocking collectives, per_device(): lax.all_to_all(packed.reshape(space, 2 * CAP, nz), 'space', 0, 0, tiled=T...  18.9 us
    pallas_call x6, Pallas kernels, call(): pl.pallas_call(kernel, out_shape=outs, in_specs=[smem if a is sig else hb...  12.7 us
    all_to_all x1, blocking collectives, per_device(): lax.all_to_all(grad.reshape(groups, count, nz), 'src', 0, 0, tiled=True)  10.4 us
    ppermute x1, starting transfers between devices, per_device(): lax.ppermute(traces_for(True), 'space', [(i, i ^ 1) for i in range(space)])  5.6 us
    ppermute x1, starting transfers between devices, per_device(): lax.ppermute(traces_for(False), 'space', [(i, (i - 1 if i % 2 == 0 else i...  4.37 us
  transfers between devices with their start and end apart: 2, of which 0 were waited for; matrix products, arithmetic and copies ran while one was open for 0% of the time, Pallas kernels for 16%

profile of v4, /device:TPU:1, one launch (start us, length us, event | category | flops | bytes accessed | tf_op | source)
XLA Modules:
  0.0 53.0 jit_solution(15316047032586684504)
XLA Ops:
  0.0 0.0 copy-start.1
  0.0 1.6 %shard_map.56 = f32[13,64,128]{2,1,0:T(8,128)S(1)} custom-call(f32[1,3,8,64,128]{4,3,2,1,0:T(8,128)} %fwd_hbm.5, f32[1,3,8,64,128]{4,3,2,1,0:T(8,128)} %adj_hbm.5, f32[8,64,128]{2,1,0:T(8,128)} %eps.1), custom_call_target="tpu_custom_call" | custom-call | tf_op jit(solution)/shard_map/pallas_call | solution.py:429
  1.6 0.0 copy-start
  1.6 4.4 %collective-permute-start = (f32[13,64,128]{2,1,0:T(8,128)S(1)}, f32[13,64,128]{2,1,0:T(8,128)S(1)}, u32[]{:S(2)}, u32[]{:S(2)}) collective-permute-start(f32[13,64,128]{2,1,0:T(8,128)S(1)} %shard_map.56), channel_id=1, source_target_pairs={{0,31},{1,2},{2,1},{3,4},{4,3},{5,6},{6,5},{7,8},{8,7},{9,10},{10,... | collective-permute-start | bytes 1277960 | tf_op jit(solution)/shard_map/ppermute | solution.py:456
  6.0 1.5 %shard_map.57 = f32[13,64,128]{2,1,0:T(8,128)S(1)} custom-call(f32[1,3,8,64,128]{4,3,2,1,0:T(8,128)} %fwd_hbm.5, f32[1,3,8,64,128]{4,3,2,1,0:T(8,128)} %adj_hbm.5, f32[8,64,128]{2,1,0:T(8,128)} %eps.1), custom_call_target="tpu_custom_call" | custom-call | tf_op jit(solution)/shard_map/pallas_call | solution.py:429
  7.4 5.6 %collective-permute-start.1 = (f32[13,64,128]{2,1,0:T(8,128)S(1)}, f32[13,64,128]{2,1,0:T(8,128)S(1)}, u32[]{:S(2)}, u32[]{:S(2)}) collective-permute-start(f32[13,64,128]{2,1,0:T(8,128)S(1)} %shard_map.57), channel_id=1, source_target_pairs={{0,1},{1,0},{2,3},{3,2},{4,5},{5,4},{6,7},{7,6},{8,9},{9,8},{10,11... | collective-permute-start | bytes 1277960 | tf_op jit(solution)/shard_map/ppermute | solution.py:455
  13.7 0.1 add_convert_fusion
  13.8 0.1 pad_maximum_fusion.sig
  13.9 0.0 copy-done.1
  13.9 7.0 %shard_map.55 = (f32[8,8,8,128]{3,2,1,0:T(8,128)S(1)}, f32[2,8,64,128]{3,2,1,0:T(8,128)S(1)}, f32[2,2,6,3,64,128]{5,4,3,2,1,0:T(8,128)S(1)}, bf16[256,256]{1,0:T(8,128)(2,1)S(1)}, bf16[64,128]{1,0:T(8,128)(2,1)S(1)}) custom-call(f32[10]{0:T(128)S(1)} %pad_maximum_fusion.sig, f32[1,3,8,64,128]{4,3,2,1,0:T(8,128)} %fwd_hbm.5, f32[1,3,8,64,128]{4,3,2,1,0:T(8,128)} %adj_hbm.5, ...), custom_call_target="tpu_custom_call" | custom-call | tf_op jit(solution)/shard_map/pallas_call | solution.py:429
  20.9 0.0 collective-permute-done.from_ring
  20.9 0.0 collective-permute-done.1.from_chip
  20.9 0.0 copy-done
  21.0 1.7 %shard_map.58 = f32[8,8,8,128]{3,2,1,0:T(8,128)S(1)} custom-call(f32[10]{0:T(128)S(1)} %pad_maximum_fusion.sig, f32[8,64,128]{2,1,0:T(8,128)S(1)} %copy-done, f32[8,8,8,128]{3,2,1,0:T(8,128)S(1)} %get-tuple-element.10.grad, f32[2,8,64,128]{3,2,1,0:T(8,128)S(1)} %get-tuple-element.11.near, f32[2,2,6,3,64,128]{5,4,3,2,1,0:T(8,128)S(1)} %get-tuple-element.12.mixes, ...), custom_call_target="tpu_custom_call" | custom-call | tf_op jit(solution)/shard_map/pallas_call | solution.py:429
  22.6 10.4 %all_to_all.10.parts = f32[8,64,128]{2,1,0:T(8,128)S(1)} all-to-all(f32[8,64,128]{2,1,0:T(8,128)S(1)} %bitcast.6), channel_id=1, replica_groups=mesh['src'=8,'space'=32] {'src'}, dimensions={0} | all-to-all | bytes 524288 | tf_op jit(solution)/shard_map/all_to_all | solution.py:486
  33.0 0.2 shard_map.59
  33.2 18.9 %all_to_all.11 = f32[32,8,128]{2,1,0:T(8,128)S(1)} all-to-all(f32[32,8,128]{2,1,0:T(8,128)S(1)} %bitcast.8), channel_id=1, replica_groups=mesh['src'=8,'space'=32] {'space'}, dimensions={0} | all-to-all | bytes 262144 | tf_op jit(solution)/shard_map/all_to_all | solution.py:488
  52.1 0.8 %shard_map.60 = f32[16,128]{1,0:T(8,128)} custom-call(f32[256,128]{1,0:T(8,128)S(1)} %bitcast.7), custom_call_target="tpu_custom_call" | custom-call | tf_op jit(solution)/shard_map/pallas_call | solution.py:429
  (1 shorter events, 0.0 us)
Async XLA Ops:
  0.0 13.9 %copy-start.1 = (s32[8,8]{1,0:T(8,128)S(1)}, s32[8,8]{1,0:T(8,128)}, u32[]{:S(2)}) copy-start(s32[8,8]{1,0:T(8,128)} %footprint.1) | copy-start | bytes 772
  1.6 19.4 %copy-start = (f32[8,64,128]{2,1,0:T(8,128)S(1)}, f32[8,64,128]{2,1,0:T(8,128)}, u32[]{:S(2)}) copy-start(f32[8,64,128]{2,1,0:T(8,128)} %eps.1) | copy-start | bytes 786436
  1.6 19.3 %collective-permute-start = (f32[13,64,128]{2,1,0:T(8,128)S(1)}, f32[13,64,128]{2,1,0:T(8,128)S(1)}, u32[]{:S(2)}, u32[]{:S(2)}) collective-permute-start(f32[13,64,128]{2,1,0:T(8,128)S(1)} %shard_map.56), channel_id=1, source_target_pairs={{0,31},{1,2},{2,1},{3,4},{4,3},{5,6},{6,5},{7,8},{8,7},{9,10},{10,... | collective-permute-start | bytes 1277960 | tf_op jit(solution)/shard_map/ppermute | solution.py:456
  7.4 13.5 %collective-permute-start.1 = (f32[13,64,128]{2,1,0:T(8,128)S(1)}, f32[13,64,128]{2,1,0:T(8,128)S(1)}, u32[]{:S(2)}, u32[]{:S(2)}) collective-permute-start(f32[13,64,128]{2,1,0:T(8,128)S(1)} %shard_map.57), channel_id=1, source_target_pairs={{0,1},{1,0},{2,3},{3,2},{4,5},{5,4},{6,7},{7,6},{8,9},{9,8},{10,11... | collective-permute-start | bytes 1277960 | tf_op jit(solution)/shard_map/ppermute | solution.py:455

commit v5 on v4

--- a/solution.py
+++ b/solution.py
@@ -237,7 +237,7 @@
 
     wide, width = footprint.shape
     count = wide * width
-    owners = put.shape[0] // (2 * CAP)
+    owners = put.shape[0] // (CAP + 1)
     ids = footprint[...]
     by_row = jnp.concatenate(
         [jnp.broadcast_to(ids[i : i + 1], (width, width)) for i in range(wide)], axis=0
@@ -250,19 +250,17 @@
     )
     row = jnp.sum(jnp.where(diagonal, col, 0.0), axis=0, keepdims=True)
     row, col = row.astype(jnp.int32), col.astype(jnp.int32)
-    lanes = lax.broadcasted_iota(jnp.int32, pixel.shape, 1)
-    pixel[...] = ((col & (PIX_DEV - 1)) == lanes).astype(F32).astype(BF16)
     row_owner = (row >> 4) & (owners - 1)
     col_owner = (col >> 4) & (owners - 1)
-    earlier = lax.broadcasted_iota(jnp.int32, (count, count), 0) < lax.broadcasted_iota(
-        jnp.int32, (count, count), 1
-    )
-    same = (row_owner == col_owner) & earlier
-    rank = jnp.sum(same.astype(F32), axis=0, keepdims=True).astype(jnp.int32)
-    slot = row_owner * (2 * CAP) + rank
+    one, two = (lax.broadcasted_iota(jnp.int32, (count, count), axis) for axis in range(2))
+    same = (row_owner == col_owner).astype(F32)
+    row_rank = jnp.sum(jnp.where(one < two, same, 0.0), axis=0, keepdims=True).astype(jnp.int32)
+    col_rank = jnp.sum(jnp.where(two < one, same, 0.0), axis=1, keepdims=True).astype(jnp.int32)
+    lanes = lax.broadcasted_iota(jnp.int32, pixel.shape, 1)
+    pixel[...] = ((col & (PIX_DEV - 1)) + col_rank * PIX_DEV == lanes).astype(F32).astype(BF16)
     rows = lax.broadcasted_iota(jnp.int32, (put.shape[0], count), 0)
-    value = (rows == slot).astype(F32)
-    mark = (rows == slot + CAP).astype(F32)
+    value = (rows == row_rank * owners + row_owner).astype(F32)
+    mark = (rows == CAP * owners + row_owner).astype(F32)
     put[...] = jnp.concatenate([value, value, value, mark], axis=1).astype(BF16)
 
 
@@ -384,14 +382,22 @@
     for s in range(1, parts.shape[0]):
         summed = summed + parts[s]
     rows = jnp.concatenate([*in_thirds(summed), pixel[...]], axis=0)
-    out[...] = jnp.dot(put[...], rows, preferred_element_type=F32)
+    packed = jnp.dot(put[...], rows, preferred_element_type=F32)
+    owners, _, width = out.shape
+    depth = width // (CAP + 1)
+    for j in range(CAP + 1):
+        out[:, 0, j * depth : (j + 1) * depth] = packed[j * owners : (j + 1) * owners]
 
 
 def pixel_kernel(arrived, out):
-    got = arrived[...]
-    rows = lax.broadcasted_iota(jnp.int32, got.shape, 0)
-    is_data = (rows & (2 * CAP - 1)) < CAP
-    pixel = jnp.where(is_data, pltpu.roll(got, got.shape[0] - CAP, 0), 0.0).astype(BF16)
+    depth = out.shape[1]
+    marks = arrived[:, 0, CAP * depth :]
+    pixel = jnp.concatenate(
+        [marks] + [pltpu.roll(marks, depth - j * PIX_DEV, 1) for j in range(1, CAP)], axis=0
+    ).astype(BF16)
+    got = jnp.concatenate(
+        [arrived[:, 0, j * depth : (j + 1) * depth] for j in range(CAP)], axis=0
+    )
     sums = None
     for part in in_thirds(got):
         sums = add(
@@ -464,7 +470,7 @@
             array(groups, planes, width, nz),
             array(2, 8, ny, nz),
             array(2, 2, len(REACHED), 3, ny, nz),
-            array(space * 2 * CAP, 4 * count, dtype=BF16),
+            array(space * (CAP + 1), 4 * count, dtype=BF16),
             array(count, nz, dtype=BF16),
         ),
         20,
@@ -484,11 +490,11 @@
         (sig, inv_eps, grad, near, mixes, from_ring, from_chip),
     )
     parts = lax.all_to_all(grad.reshape(groups, count, nz), "src", 0, 0, tiled=True)
-    (packed,) = call(pack_kernel, (array(space * 2 * CAP, nz),), 4, (parts, put, pixel))
-    arrived = lax.all_to_all(packed.reshape(space, 2 * CAP, nz), "space", 0, 0, tiled=True)
-    (sums,) = call(
-        pixel_kernel, (array(PIX_DEV, nz),), 4, (arrived.reshape(space * 2 * CAP, nz),)
-    )
+    (packed,) = call(
+        pack_kernel, (array(space, 1, (CAP + 1) * nz),), 4, (parts, put, pixel)
+    )
+    arrived = lax.all_to_all(packed, "space", 0, 0, tiled=True)
+    (sums,) = call(pixel_kernel, (array(PIX_DEV, nz),), 4, (arrived,))
     return sums
 
 

time: 53.2 us -> 52.5 us (0.987)
  blocking collectives: 29.3 us -> 28.5 us
    all_to_all x1, blocking collectives: 18.9 us -> 18.1 us  [per_device(): arrived = lax.all_to_all(packed, 'space', 0, 0, tiled=True)]
where the time goes in v5:
time: 52.5 us; the launch traced here: 52.3 us
  blocking collectives  28.5 us (54%)
  Pallas kernels  12.8 us (24%)
  starting transfers between devices  9.97 us (19%)
  between operations  0.73 us (1%)
    all_to_all x1, blocking collectives, per_device(): arrived = lax.all_to_all(packed, 'space', 0, 0, tiled=True)  18.1 us
    pallas_call x6, Pallas kernels, call(): pl.pallas_call(kernel, out_shape=outs, in_specs=[smem if a is sig else hb...  12.8 us
    all_to_all x1, blocking collectives, per_device(): lax.all_to_all(grad.reshape(groups, count, nz), 'src', 0, 0, tiled=True)  10.4 us
    ppermute x1, starting transfers between devices, per_device(): lax.ppermute(traces_for(True), 'space', [(i, i ^ 1) for i in range(space)])  5.6 us
    ppermute x1, starting transfers between devices, per_device(): lax.ppermute(traces_for(False), 'space', [(i, (i - 1 if i % 2 == 0 else i...  4.37 us
  transfers between devices with their start and end apart: 2, of which 0 were waited for; matrix products, arithmetic and copies ran while one was open for 0% of the time, Pallas kernels for 16%

profile of v5, /device:TPU:1, one launch (start us, length us, event | category | flops | bytes accessed | tf_op | source)
XLA Modules:
  0.0 52.3 jit_solution(2577960645935692707)
XLA Ops:
  0.0 0.0 copy-start.1
  0.0 1.6 %shard_map.56 = f32[13,64,128]{2,1,0:T(8,128)S(1)} custom-call(f32[1,3,8,64,128]{4,3,2,1,0:T(8,128)} %fwd_hbm.5, f32[1,3,8,64,128]{4,3,2,1,0:T(8,128)} %adj_hbm.5, f32[8,64,128]{2,1,0:T(8,128)} %eps.1), custom_call_target="tpu_custom_call" | custom-call | tf_op jit(solution)/shard_map/pallas_call | solution.py:435
  1.6 0.0 copy-start
  1.6 4.4 %collective-permute-start = (f32[13,64,128]{2,1,0:T(8,128)S(1)}, f32[13,64,128]{2,1,0:T(8,128)S(1)}, u32[]{:S(2)}, u32[]{:S(2)}) collective-permute-start(f32[13,64,128]{2,1,0:T(8,128)S(1)} %shard_map.56), channel_id=1, source_target_pairs={{0,31},{1,2},{2,1},{3,4},{4,3},{5,6},{6,5},{7,8},{8,7},{9,10},{10,... | collective-permute-start | bytes 1277960 | tf_op jit(solution)/shard_map/ppermute | solution.py:462
  6.0 1.5 %shard_map.57 = f32[13,64,128]{2,1,0:T(8,128)S(1)} custom-call(f32[1,3,8,64,128]{4,3,2,1,0:T(8,128)} %fwd_hbm.5, f32[1,3,8,64,128]{4,3,2,1,0:T(8,128)} %adj_hbm.5, f32[8,64,128]{2,1,0:T(8,128)} %eps.1), custom_call_target="tpu_custom_call" | custom-call | tf_op jit(solution)/shard_map/pallas_call | solution.py:435
  7.4 5.6 %collective-permute-start.1 = (f32[13,64,128]{2,1,0:T(8,128)S(1)}, f32[13,64,128]{2,1,0:T(8,128)S(1)}, u32[]{:S(2)}, u32[]{:S(2)}) collective-permute-start(f32[13,64,128]{2,1,0:T(8,128)S(1)} %shard_map.57), channel_id=1, source_target_pairs={{0,1},{1,0},{2,3},{3,2},{4,5},{5,4},{6,7},{7,6},{8,9},{9,8},{10,11... | collective-permute-start | bytes 1277960 | tf_op jit(solution)/shard_map/ppermute | solution.py:461
  13.7 0.1 add_convert_fusion
  13.8 0.1 pad_maximum_fusion.sig
  13.9 0.0 copy-done.1
  13.9 7.0 %shard_map.55 = (f32[8,8,8,128]{3,2,1,0:T(8,128)S(1)}, f32[2,8,64,128]{3,2,1,0:T(8,128)S(1)}, f32[2,2,6,3,64,128]{5,4,3,2,1,0:T(8,128)S(1)}, bf16[160,256]{1,0:T(8,128)(2,1)S(1)}, bf16[64,128]{1,0:T(8,128)(2,1)S(1)}) custom-call(f32[10]{0:T(128)S(1)} %pad_maximum_fusion.sig, f32[1,3,8,64,128]{4,3,2,1,0:T(8,128)} %fwd_hbm.5, f32[1,3,8,64,128]{4,3,2,1,0:T(8,128)} %adj_hbm.5, ...), custom_call_target="tpu_custom_call" | custom-call | tf_op jit(solution)/shard_map/pallas_call | solution.py:435
  20.9 0.0 collective-permute-done.from_ring
  20.9 0.0 collective-permute-done.1.from_chip
  21.0 0.0 copy-done
  21.0 1.7 %shard_map.58 = f32[8,8,8,128]{3,2,1,0:T(8,128)S(1)} custom-call(f32[10]{0:T(128)S(1)} %pad_maximum_fusion.sig, f32[8,64,128]{2,1,0:T(8,128)S(1)} %copy-done, f32[8,8,8,128]{3,2,1,0:T(8,128)S(1)} %get-tuple-element.10.grad, f32[2,8,64,128]{3,2,1,0:T(8,128)S(1)} %get-tuple-element.11.near, f32[2,2,6,3,64,128]{5,4,3,2,1,0:T(8,128)S(1)} %get-tuple-element.12.mixes, ...), custom_call_target="tpu_custom_call" | custom-call | tf_op jit(solution)/shard_map/pallas_call | solution.py:435
  22.7 10.4 %all_to_all.10.parts = f32[8,64,128]{2,1,0:T(8,128)S(1)} all-to-all(f32[8,64,128]{2,1,0:T(8,128)S(1)} %bitcast.4), channel_id=1, replica_groups=mesh['src'=8,'space'=32] {'src'}, dimensions={0} | all-to-all | bytes 524288 | tf_op jit(solution)/shard_map/all_to_all | solution.py:492
  33.0 0.2 shard_map.59
  33.3 18.1 %all_to_all.11.arrived = f32[32,1,640]{2,1,0:T(1,128)S(1)} all-to-all(f32[32,1,640]{2,1,0:T(1,128)S(1)} %shard_map.59), channel_id=1, replica_groups=mesh['src'=8,'space'=32] {'space'}, dimensions={0} | all-to-all | bytes 163840 | tf_op jit(solution)/shard_map/all_to_all | solution.py:496
  51.4 0.9 %shard_map.60 = f32[16,128]{1,0:T(8,128)} custom-call(f32[32,1,640]{2,1,0:T(1,128)S(1)} %all_to_all.11.arrived), custom_call_target="tpu_custom_call" | custom-call | tf_op jit(solution)/shard_map/pallas_call | solution.py:435
  (1 shorter events, 0.0 us)
Async XLA Ops:
  0.0 13.9 %copy-start.1 = (s32[8,8]{1,0:T(8,128)S(1)}, s32[8,8]{1,0:T(8,128)}, u32[]{:S(2)}) copy-start(s32[8,8]{1,0:T(8,128)} %footprint.1) | copy-start | bytes 772
  1.6 19.4 %copy-start = (f32[8,64,128]{2,1,0:T(8,128)S(1)}, f32[8,64,128]{2,1,0:T(8,128)}, u32[]{:S(2)}) copy-start(f32[8,64,128]{2,1,0:T(8,128)} %eps.1) | copy-start | bytes 786436
  1.6 19.3 %collective-permute-start = (f32[13,64,128]{2,1,0:T(8,128)S(1)}, f32[13,64,128]{2,1,0:T(8,128)S(1)}, u32[]{:S(2)}, u32[]{:S(2)}) collective-permute-start(f32[13,64,128]{2,1,0:T(8,128)S(1)} %shard_map.56), channel_id=1, source_target_pairs={{0,31},{1,2},{2,1},{3,4},{4,3},{5,6},{6,5},{7,8},{8,7},{9,10},{10,... | collective-permute-start | bytes 1277960 | tf_op jit(solution)/shard_map/ppermute | solution.py:462
  7.4 13.5 %collective-permute-start.1 = (f32[13,64,128]{2,1,0:T(8,128)S(1)}, f32[13,64,128]{2,1,0:T(8,128)S(1)}, u32[]{:S(2)}, u32[]{:S(2)}) collective-permute-start(f32[13,64,128]{2,1,0:T(8,128)S(1)} %shard_map.57), channel_id=1, source_target_pairs={{0,1},{1,0},{2,3},{3,2},{4,5},{5,4},{6,7},{7,6},{8,9},{9,8},{10,11... | collective-permute-start | bytes 1277960 | tf_op jit(solution)/shard_map/ppermute | solution.py:461
